TPU v7x, 256 devices: a whole 4x4x8 slice. The times are simulated.
256 devices in a mesh: dp: 8 (over x, core), tm: 8 (over z), space: 4 (over y).
Axes of the slice: x: 4, y: 4, z: 8, core: 2. Of those that a mesh axis runs over, the one named last changes fastest.
Arguments:
- latents: bfloat16 [8, 16, 8, 128, 512], P('dp', 'tm', 'space'), may hold values from -400 to 400
- owner: int32 [8, 4, 1], P('dp'), may hold values from 0 to 3; in each aligned block of 4 rows (0 to 3, 4 to 7, ..., all dimensions but the last counted through in order) at most 2 rows name the same one
- gamma: float32 [512], replicated, may hold values from 0.25 to 1.75
- beta: float32 [512], replicated, may hold values from -3 to 3
- weight: bfloat16 [512, 27, 256], P(('dp', 'tm', 'space')), may hold values from -0.0546875 to 0.0546875
- upstream: bfloat16 [8, 16, 4, 512, 256], P('dp', 'tm', 'space'), may hold values from -20 to 20
Outputs:
- dlatents: bfloat16 [8, 16, 8, 128, 512], P('dp', 'tm', 'space')
- dweight: float32 [512, 27, 256], P(('dp', 'tm', 'space'))
- dgamma: float32 [512], replicated
- dbeta: float32 [512], replicated
Inputs may be any that keep to these rules, and one draw needn't show every extreme that they name: `owner`: in every clip each of the 4 owners is named by at most 2 of the 4 tiles, and by exactly 2 in some clips.
All inputs are finite; a program needn't handle non-finite values.
Results may differ from a plain program's by a relative error of at most 0.002.
The roundings to bfloat16 on the way count: a program that leaves them out, or rounds other values in their place, can miss the bound.
Values may be sent and summed in bfloat16 or wider, within the bound.
A program may use at most 128 MiB of HBM per device.

v0:
```python
import math

import jax
import jax.numpy as jnp
from jax import lax
from jax.sharding import PartitionSpec as P

GROUPS = 32
TH = 8
TW = 16


EPS = 1e-06


def shifted(value, axis, steps):
    count = lax.axis_size(axis)
    initial, last = (max(0, -steps), min(count, count - steps))
    return lax.ppermute(value, axis, [(source, source + steps) for source in range(initial, last)])


def tap_list():
    return [(kt, ky, kx) for kt in range(3) for ky in range(3) for kx in range(3)]


def conv_grads(hidden, grads, weight, rscale):
    frames, count, cells, chans = hidden.shape
    outs_ch = grads.shape[3]
    first_dev = lax.axis_index("tm") == 0
    cache = shifted(hidden, "tm", 1)
    repeat = jnp.concatenate([hidden[:1], hidden[:1]], axis=0)
    cache = jnp.where(first_dev, repeat, cache)
    extended = jnp.concatenate([cache, hidden], axis=0).reshape(frames + 2, count, TH, TW, chans)
    padded = jnp.pad(extended, ((0, 0), (0, 0), (1, 1), (1, 1), (0, 0)))
    rows = grads.reshape(frames * count * cells, outs_ch)
    span = lax.axis_size(("dp", "tm", "space")) * weight.shape[0]
    terms = []
    for kt, ky, kx in tap_list():
        tap = padded[kt : kt + frames, :, ky : ky + TH, kx : kx + TW].reshape(
            frames * count * cells, span
        )
        terms.append(
            lax.dot_general(tap, rows, (((0,), (0,)), ((), ())), preferred_element_type=jnp.float32)
        )
    dweight = lax.psum_scatter(
        jnp.stack(terms, axis=1) * rscale, ("dp", "tm", "space"), scatter_dimension=0, tiled=True
    )
    piece = lax.all_gather(weight, ("dp", "tm", "space"), axis=0, tiled=True)
    span = piece.shape[0]
    total = jnp.zeros((frames + 2, count, TH + 2, TW + 2, span), jnp.float32)
    for index, (kt, ky, kx) in enumerate(tap_list()):
        back = lax.dot_general(
            rows, piece[:, index, :], (((1,), (1,)), ((), ())), preferred_element_type=jnp.float32
        )
        total = total.at[kt : kt + frames, :, ky : ky + TH, kx : kx + TW].add(
            back.reshape(frames, count, TH, TW, span)
        )
    dextended = total[:, :, 1 : TH + 1, 1 : TW + 1].reshape(frames + 2, count, cells, span)
    carried = shifted(dextended[:2].astype(jnp.bfloat16), "tm", -1).astype(jnp.float32)
    own_part = dextended[2:]
    own_part = own_part.at[frames - 2 :].add(carried)
    own_part = own_part.at[0].add(jnp.where(first_dev, dextended[0] + dextended[1], 0.0))
    return (own_part, dweight)


def shards(latents, owner, gamma, beta, weight, upstream):
    blocks = latents[0]
    frames, cap, cells, chans = blocks.shape
    spaces = lax.axis_size("space")
    here = lax.axis_index("space")
    per_dev = upstream.shape[2]
    outs_ch = upstream.shape[4]
    tile_ids = owner[0, :, 0]
    tiles = tile_ids.shape[0]
    width = chans // GROUPS
    hot = (tile_ids[:, None] == jnp.arange(spaces, dtype=jnp.int32)[None, :]).astype(jnp.int32)
    rank = jnp.sum((jnp.cumsum(hot, axis=0) - hot) * hot, axis=1)
    slot = tile_ids * cap + rank
    holds = slot[None, :] == (here * cap + jnp.arange(cap, dtype=jnp.int32))[:, None]
    live = jnp.any(holds, axis=1).astype(jnp.float32)
    tile_of = jnp.sum(holds.astype(jnp.int32) * jnp.arange(tiles, dtype=jnp.int32)[None, :], axis=1)
    frames_all = frames * lax.axis_size("tm")
    count = float(frames_all * tiles * cells * width)
    rscale = 1.0 / math.sqrt(lax.axis_size("dp") * frames_all * tiles * cells)
    values = blocks.astype(jnp.float32).reshape(frames, cap, cells, GROUPS, width)
    live_mask = live[None, :, None, None, None]
    total = lax.psum(jnp.sum(values * live_mask, axis=(0, 1, 2, 4)), ("tm", "space"))
    mean = total / count
    centred = values - mean[:, None]
    spread = lax.psum(jnp.sum(centred * centred * live_mask, axis=(0, 1, 2, 4)), ("tm", "space"))
    var = spread / count
    inverse = lax.rsqrt(var + EPS)
    normed = (centred * inverse[:, None]).reshape(frames, cap, cells, chans)
    act = normed * gamma + beta
    sig = jax.nn.sigmoid(act)
    hidden = (act * sig).astype(jnp.bfloat16)
    ups = upstream[0].astype(jnp.float32).reshape(frames, per_dev, TH, 2, TW, 2, outs_ch)
    pooled = jnp.sum(ups, axis=(3, 5)).reshape(frames, per_dev, cells, outs_ch).astype(jnp.bfloat16)
    all_pooled = lax.all_gather(pooled, "space", axis=1, tiled=True)
    live_slot = live[None, :, None, None] > 0.5
    grads = jnp.where(live_slot, all_pooled[:, tile_of], jnp.zeros((), jnp.bfloat16))
    dhidden, dweight = conv_grads(hidden, grads, weight, rscale)
    dact = dhidden * (sig * (1.0 + act * (1.0 - sig))) * live[None, :, None, None]
    dgamma, dbeta = lax.psum(
        (jnp.sum(dact * normed, axis=(0, 1, 2)) * rscale, jnp.sum(dact, axis=(0, 1, 2)) * rscale),
        ("dp", "tm", "space"),
    )
    dnorm = (dact * gamma).reshape(frames, cap, cells, GROUPS, width)
    ngroup = normed.reshape(frames, cap, cells, GROUPS, width)
    first_m, second_m = lax.psum(
        (jnp.sum(dnorm, axis=(0, 1, 2, 4)), jnp.sum(dnorm * ngroup, axis=(0, 1, 2, 4))),
        ("tm", "space"),
    )
    dvalues = inverse[:, None] * (
        dnorm - (first_m / count)[:, None] - ngroup * (second_m / count)[:, None]
    )
    dfull = dvalues.reshape(frames, cap, cells, chans)
    resid = jnp.pad(grads.astype(jnp.float32), ((0, 0), (0, 0), (0, 0), (0, chans - outs_ch)))
    dlatent = ((dfull + resid) * live[None, :, None, None]).astype(jnp.bfloat16)
    return (dlatent[None], dweight, dgamma, dbeta)


def solution(mesh):
    return jax.shard_map(
        shards,
        mesh=mesh,
        in_specs=(
            P("dp", "tm", "space", None, None),
            P("dp", None, None),
            P(),
            P(),
            P(("dp", "tm", "space"), None, None),
            P("dp", "tm", "space", None, None),
        ),
        out_specs=(
            P("dp", "tm", "space", None, None),
            P(("dp", "tm", "space"), None, None),
            P(),
            P(),
        ),
        check_vma=False,
    )
```

profile of v0, /device:TPU:1, one launch (start us, length us, event | category | flops | bytes accessed | tf_op | source)
XLA Modules:
  0.0 779.9 jit_solution(5624047049725243167)
XLA Ops:
  13.3 12.6 %all_gather.6 = bf16[2,4,128,256]{3,2,1,0:T(8,128)(2,1)S(1)} all-gather(bf16[2,1,128,256]{3,2,1,0:T(8,128)(2,1)S(1)} %bitcast.575), channel_id=1, replica_groups=mesh['dp'=8,'tm'=8,'space'=4] {'space'}, dimensions={1}, use_global_device_ids=true | all-gather | bytes 655360 | tf_op jit(solution)/shard_map/all_gather | solution.py:99
  28.7 62.6 %psum.42 = f32[32]{0:T(128)S(1)} all-reduce(f32[32]{0:T(128)S(1)} %reduce_sum.114), channel_id=1, replica_groups=mesh['dp'=8,'tm'=8,'space'=4] {'tm','space'}, use_global_device_ids=true, to_apply=%region_5.6 | all-reduce | flops 32 | bytes 256 | tf_op jit(solution)/shard_map/psum | solution.py:87
  93.7 41.3 %all-gather.2.cloned.1.call-done = bf16[512,27,256]{2,1,0:T(8,128)(2,1)} async-done(((bf16[2,27,256]{2,1,0:T(8,128)(2,1)}), bf16[512,27,256]{2,1,0:T(8,128)(2,1)}) %all-gather.2.cloned.1.call-update) | async-done | bytes 7077904 | tf_op jit(solution)/shard_map/all_gather | solution.py:48
  135.0 10.9 %fusion.73 = (bf16[512,1,256]{2,1,0:T(2,128)(2,1)S(1)}, bf16[512,1,256]{2,1,0:T(2,128)(2,1)S(1)}, bf16[512,1,256]{2,1,0:T(2,128)(2,1)}, bf16[512,1,256]{2,1,0:T(...) fusion(bf16[512,27,256]{2,1,0:T(8,128)(2,1)} %all-gather.2.clon, ...), kind=kLoop, calls=%fused_computation.207 | loop fusion | bytes 4194304 | tf_op jit(solution)/shard_map/slice | solution.py:53
  149.0 5.8 scatter-add.95
  156.7 5.8 scatter-add.96
  162.5 2.8 fusion.7
  167.2 5.8 scatter-add.100
  172.9 3.9 add_select_fusion
  176.8 7.1 scatter-add.101
  188.3 5.8 scatter-add.105
  194.1 21.0 %fusion.72 = (bf16[512,1,256]{2,1,0:T(2,128)(2,1)S(1)}, bf16[512,1,256]{2,1,0:T(2,128)(2,1)S(1)}, bf16[512,1,256]{2,1,0:T(2,128)(2,1)}, bf16[512,1,256]{2,1,0:T(...) fusion(bf16[512,27,256]{2,1,0:T(8,128)(2,1)} %all-gather.2.clon, ...), kind=kLoop, calls=%fused_computation.206 | loop fusion | bytes 9961472 | tf_op jit(solution)/shard_map/slice | solution.py:53
  216.8 5.8 scatter-add.106
  227.2 5.8 scatter-add.110
  234.9 5.8 scatter-add.111
  245.4 5.8 scatter-add.115
  253.1 6.0 scatter-add.116
  263.7 5.8 scatter-add.120
  271.3 5.8 scatter-add.121
  281.8 5.8 scatter-add.125
  289.5 5.8 scatter-add.126
  300.0 5.8 scatter-add.130
  307.7 5.8 scatter-add.131
  318.0 5.8 scatter-add.135
  325.6 5.8 scatter-add.136
  335.8 60.9 %psum.43 = f32[32]{0:T(128)S(1)} all-reduce(f32[32]{0:T(128)S(1)} %reduce_sum.117), channel_id=1, replica_groups=mesh['dp'=8,'tm'=8,'space'=4] {'tm','space'}, use_global_device_ids=true, to_apply=%region_8.9 | all-reduce | flops 32 | bytes 256 | tf_op jit(solution)/shard_map/psum | solution.py:90
  405.0 6.0 collective-permute-done.1
  414.5 3.1 pad_slice_fusion
  448.6 11.5 %broadcast_multiply_fusion = f32[512,27,256]{2,0,1:T(8,128)} fusion(f32[512,27,256]{2,0,1:T(8,128)} %fusion.9), kind=kLoop, calls=%fused_computation.25 | loop fusion | flops 3538944 | bytes 28311552 | tf_op jit(solution)/shard_map/mul | solution.py:46
  460.6 58.2 %all-reduce.5 = (f32[32]{0:T(128)S(1)}, f32[32]{0:T(128)S(1)}) all-reduce(f32[32]{0:T(128)S(1)} %reduce_sum.126, f32[32]{0:T(128)S(1)} %reduce_sum.123), channel_id=1, replica_groups=mesh['dp'=8,'tm'=8,'space'=4] {'tm','space'}, use_global_device_ids=true, to_apply=%region_17.18 | all-reduce | flops 64 | bytes 512 | tf_op jit(solution)/shard_map/psum | solution.py:110
  520.6 108.4 %all-reduce.4 = (f32[512]{0:T(512)}, f32[512]{0:T(512)}) all-reduce(f32[512]{0:T(512)S(1)} %get-tuple-element.442, f32[512]{0:T(512)S(1)} %get-tuple-element.441), channel_id=1, replica_groups=mesh['dp'=8,'tm'=8,'space'=4] {'dp','tm','space'}, use_global_device_ids=true, to_apply=%region_20.21 | all-reduce | flops 1024 | bytes 8192 | tf_op jit(solution)/shard_map/psum | solution.py:104
  629.0 142.2 %all-reduce.8.cloned.1.call-done = f32[512,27,256]{2,0,1:T(8,128)} async-done(((f32[512,27,256]{2,0,1:T(8,128)}), f32[512,27,256]{2,0,1:T(8,128)}) %all-reduce.8.cloned.1.call-update) | async-done | bytes 14155792
  (129 shorter events, 114.0 us)
Async XLA Ops:
  7.2 127.8 %all-gather.2.cloned.1.call-start = ((), (), s32[]{:S(2)}) async-start(), calls=%async_computation | async-start | bytes 8421376 | tf_op jit(solution)/shard_map/all_gather | solution.py:48
  8.6 762.6 %all-reduce.8.cloned.1.call-start = ((), (), s32[]{:S(2)}) async-start(), calls=%async_computation.1 | async-start | bytes 28311552
  325.6 76.3 %copy-start.1 = (f32[512]{0:T(512)S(1)}, f32[512]{0:T(512)}, u32[]{:S(2)}) copy-start(f32[512]{0:T(512)} %param.68) | copy-start | bytes 6148
  325.6 76.3 %copy-start.2 = (f32[512]{0:T(512)S(1)}, f32[512]{0:T(512)}, u32[]{:S(2)}) copy-start(f32[512]{0:T(512)} %param.69) | copy-start | bytes 6148
  334.0 66.6 %collective-permute-start = (bf16[2,2,128,512]{2,3,1,0:T(8,128)(2,1)}, bf16[2,2,128,512]{2,3,1,0:T(8,128)(2,1)}, u32[]{:S(2)}, u32[]{:S(2)}) collective-permute-start(bf16[2,2,128,512]{2,3,1,0:T(8,128)(2,1)} %copy.128), channel_id=1, source_target_pairs={{4,0},{8,4},{12,8},{16,12},{20,16},{24,20},{28,24},{5,1},{9,5},{13... | collective-permute-start | bytes 1572872 | tf_op jit(solution)/shard_map/ppermute | solution.py:19
  403.6 7.4 collective-permute-start.1
  460.1 58.9 %copy-start = (f32[2,2,128,512]{2,3,1,0:T(8,128)S(1)}, f32[2,2,128,512]{2,3,1,0:T(8,128)}, u32[]{:S(2)}) copy-start(f32[2,2,128,512]{2,3,1,0:T(8,128)} %get-tuple-element.384) | copy-start | bytes 3145732
Sparse Core Ops, SparseCore 0:
  12.4 122.5 all-gather.1
  460.3 310.9 all-reduce.7
where the time goes:
time: 786 us; the launch traced here: 780 us
  blocking collectives  303 us (39%)
  waiting for transfers between devices  190 us (24%)
  local copies, waits for them, and re-layouts  159 us (20%)
  matrix products  87.1 us (11%)
  other arithmetic  24 us (3%)
  between operations  14.7 us (2%)
    unnamed x3, waiting for transfers between devices  142 us
    psum x1, blocking collectives, shards(): lax.psum((jnp.sum(dact * normed, axis=(0, 1, 2)) * rscale, jnp.sum(dact,...  108 us
    scatter-add x19, local copies, waits for them, and re-layouts, conv_grads(): total.at[kt:kt + frames, :, ky:ky + TH, kx:kx + TW]  108 us
    psum x1, blocking collectives, shards(): lax.psum(jnp.sum(values * live_mask, axis=(0, 1, 2, 4)), ('tm', 'space'))  62.6 us
    psum x1, blocking collectives, shards(): lax.psum(jnp.sum(centred * centred * live_mask, axis=(0, 1, 2, 4)), ('tm'...  60.9 us
    psum x1, blocking collectives, shards(): lax.psum((jnp.sum(dnorm, axis=(0, 1, 2, 4)), jnp.sum(dnorm * ngroup, axis...  58.2 us
    dot_general x27, matrix products, conv_grads(): lax.dot_general(rows, piece[:, index, :], (((1,), (1,)), ((), ())), prefe...  56.1 us
    all_gather x1, waiting for transfers between devices, conv_grads(): piece = lax.all_gather(weight, ('dp', 'tm', 'space'), axis=0, tiled=True)  41.3 us
  transfers between devices with their start and end apart: 4, of which 3 were waited for; matrix products, arithmetic and copies ran while one was open for 2% of the time, Pallas kernels for 0%

commit v1 on v0

v1 whole, which is shorter than its diff:
```python
import math

import jax
import jax.numpy as jnp
from jax import lax
from jax.experimental import pallas as pl
from jax.experimental.pallas import tpu as pltpu
from jax.sharding import PartitionSpec as P

MESH = pl.DeviceIdType.MESH
F32 = jnp.float32
BF16 = jnp.bfloat16
EPS = 1e-06

NDP, NTM, NSP = 8, 8, 4
GROUPS = 32
GS = 16
FR = 16
TILES = 4
CAP = 2
TH, TW = 8, 16
CELLS = TH * TW
C, COUT = 512, 256
TAPS = 27
ROWS = 9 * GS
LEFT = 48

B_TM, B_SP, A_SP, A_TM = 0, 8, 40, 44
L_SP, L_TM, WGT = 52, 56, 64
D_TM, D_DP, G_DP, D_SP, D_OWN, G_ALL = 72, 80, 88, 96, 100, 101
N_SEM = 133


def body(
    owner_ref, gamma_ref, beta_ref, lat_ref, ups_ref, w_ref,
    dlat_ref, dw_ref, dgb_ref,
    gz, ybuf, zsend, xbuf, wbuf, wf, wk, a9, xh, ds, dhb, rsd, dk, dsend, drecv, dsum,
    dxs, zback, tback, ysend, gown, gdp, gsum, gall, send_sem, recv_sem, own_sem,
):
    d, z, y = lax.axis_index("dp"), lax.axis_index("tm"), lax.axis_index("space")
    ahead = lambda v, r, n: lax.rem(v + r, n)
    behind = lambda v, r, n: lax.rem(v - r + n, n)
    line = (d * NTM + z) * NSP + y
    mine = y * NTM + z
    w_group = line // 8
    w_tm, w_sp = lax.rem(w_group, NTM), w_group // NTM
    w_piece = lax.rem(line, 8)
    src = lambda i: {
        "dp": mine // 4,
        "tm": 2 * lax.rem(mine, 4) + i // 4,
        "space": lax.rem(jnp.int32(i), 4) if not isinstance(i, int) else i % 4,
    }
    w_self = (w_tm == z) & (w_sp == y)
    own_piece_here = line // 8 == mine

    started = []

    def copy(a, b, n, to, m=None):
        return pltpu.make_async_remote_copy(
            src_ref=a, dst_ref=b, send_sem=send_sem.at[n], recv_sem=recv_sem.at[n if m is None else m],
            device_id=to, device_id_type=MESH,
        )

    def go(a, b, n, to, m=None):
        c = copy(a, b, n, to, m)
        c.start()
        started.append(c)
        return c

    def got(region, n):
        copy(region, region, n, {"tm": z}).wait_recv()

    barrier = pltpu.get_barrier_semaphore()

    def greet(to):
        pl.semaphore_signal(barrier, inc=1, device_id=to, device_id_type=MESH)

    for r in range(NTM):
        for q in range(NSP):
            if r or q:
                greet({"tm": ahead(z, r, NTM), "space": ahead(y, q, NSP)})
    for r in range(1, NDP):
        greet({"dp": ahead(d, r, NDP)})
    for i in range(8):
        o = src(i)

        @pl.when((8 * mine + i) != line)
        def _():
            greet(o)

    @pl.when(jnp.logical_not(own_piece_here & (w_piece == d)))
    def _():
        greet({"dp": w_piece, "tm": w_tm, "space": w_sp})

    p = lax.broadcasted_iota(jnp.int32, (CELLS, 4 * CELLS), 0)
    q = lax.broadcasted_iota(jnp.int32, (CELLS, 4 * CELLS), 1)
    pool = ((q >> 6) == (p >> 4)) & (((q & 31) >> 1) == (p & 15))
    pool = jnp.where(pool, 1.0, 0.0).astype(BF16)
    for f in range(2):
        pooled = jnp.dot(pool, ups_ref[f], preferred_element_type=F32)
        gz[2 + 2 * z + f, y] = pooled.astype(BF16)
    for f in (0, 1, FR + 2, FR + 3):
        gz[f] = jnp.zeros((TILES, CELLS, COUT), BF16)

    self_w = jnp.where(w_self, 1, 0)
    self_o = jnp.where(own_piece_here & (w_piece == d), 1, 0)
    self_s = jnp.where(own_piece_here, 1, 0)
    own_to = 8 * mine + d
    self_t = jnp.where(own_to == line, 1, 0)
    pl.semaphore_wait(barrier, NTM * NSP - 1 + NDP - 1 + 8 - self_s + 1 - self_t)

    def part_b(zo, yo, f=0, n=2):
        return gz.at[pl.ds(2 + 2 * zo + f, n), yo, pl.ds(LEFT, CELLS - LEFT)]

    def part_a(zo, yo, f=0, n=2):
        return gz.at[pl.ds(2 + 2 * zo + f, n), yo, pl.ds(0, LEFT)]

    def row_a(zo, f=0, n=2):
        return gz.at[pl.ds(2 + 2 * zo + f, n), :, pl.ds(0, LEFT)]

    zr, zl = {"tm": ahead(z, 1, NTM)}, {"tm": behind(z, 1, NTM)}
    yr, yl = {"space": ahead(y, 1, NSP)}, {"space": behind(y, 1, NSP)}
    yo_r, yo_l, yo_2 = ahead(y, 1, NSP), behind(y, 1, NSP), ahead(y, 2, NSP)

    def tm_step(region, base, h):
        frames = (dict(f=0, n=2),) * 2 if h < 4 else (dict(f=0, n=1), dict(f=1, n=1))
        for way, (to, o) in enumerate(((zr, behind(z, h - 1, NTM)), (zl, ahead(z, h - 1, NTM)))):
            a = region(o, **frames[way])
            go(a, a, base + 2 * (h - 1) + way, to)

    def tm_got(region, base, h):
        frames = (dict(f=0, n=2),) * 2 if h < 4 else (dict(f=0, n=1), dict(f=1, n=1))
        for way, o in enumerate((behind(z, h, NTM), ahead(z, h, NTM))):
            got(region(o, **frames[way]), base + 2 * (h - 1) + way)

    def sp_send(region, base, zo):
        a = region(zo, y)
        go(a, a, base, yr)
        go(a, a, base + 1, yl)

    def sp_forward(region, base, zo):
        got(region(zo, yo_l), base)
        a = region(zo, yo_l, 0, 1)
        go(a, a, base + 2, yr)
        got(region(zo, yo_r), base + 1)
        a = region(zo, yo_r, 1, 1)
        go(a, a, base + 3, yl)

    def sp_got(region, base, zo):
        got(region(zo, yo_2, 0, 1), base + 2)
        got(region(zo, yo_2, 1, 1), base + 3)

    steps = (0, -1, 1, -2, 2, -3, 3, 4)
    origin = [lax.rem(z + s + NTM, NTM) for s in steps]
    b_row = lambda zo, yo, f=0, n=2: part_b(zo, yo, f, n)
    b_tm = lambda zo, f=0, n=2: part_b(zo, y, f, n)

    for r in range(1, NSP):
        yo = ahead(y, r, NSP)
        go(
            lat_ref.at[:, :, :, pl.ds(pl.multiple_of(yo * 128, 128), 128)],
            ybuf.at[y], L_SP + r, {"space": yo},
        )
    own = pltpu.make_async_copy(
        lat_ref.at[:, :, :, pl.ds(pl.multiple_of(y * 128, 128), 128)], ybuf.at[y], own_sem.at[0]
    )
    own.start()
    tm_step(b_tm, B_TM, 1)
    sp_send(part_a, A_SP, z)
    sp_send(b_row, B_SP, origin[0])

    for r in range(NDP):
        to = {"dp": ahead(d, r, NDP), "tm": w_tm, "space": w_sp}
        c = copy(w_ref, wbuf.at[w_piece], WGT + r, to, WGT + w_piece)
        if r:
            c.start()
            started.append(c)
        else:

            @pl.when(jnp.logical_not(w_self))
            def _():
                c.start()

            @pl.when(w_self)
            def _():
                pltpu.make_async_copy(w_ref, wbuf.at[w_piece], recv_sem.at[WGT + w_piece]).start()

    sp_forward(part_a, A_SP, z)
    tm_got(b_tm, B_TM, 1)
    tm_step(b_tm, B_TM, 2)
    sp_send(b_row, B_SP + 4, origin[1])
    sp_send(b_row, B_SP + 8, origin[2])

    own.wait()
    for r in range(1, NSP):
        got(ybuf.at[behind(y, r, NSP)], L_SP + r)
    owners = [owner_ref[0, t, 0] for t in range(TILES)]
    ranks = [
        jnp.minimum(
            sum([(owners[u] == owners[t]).astype(jnp.int32) for u in range(t)], jnp.int32(0)), CAP - 1
        )
        for t in range(TILES)
    ]
    for t in range(TILES):
        for f in range(2):
            v = ybuf[owners[t], f, ranks[t]].astype(F32)
            zsend[:, f * TILES + t] = v.T.reshape(NTM, GS, CELLS).astype(BF16)
    for r in range(1, NTM):
        zo = ahead(z, r, NTM)
        go(zsend.at[zo], xbuf.at[z], L_TM + r, {"tm": zo})
    xbuf[z] = zsend[z]

    sp_got(part_a, A_SP, z)
    tm_step(row_a, A_TM, 1)
    sp_forward(b_row, B_SP, origin[0])
    tm_got(b_tm, B_TM, 2)
    tm_step(b_tm, B_TM, 3)
    sp_send(b_row, B_SP + 12, origin[3])
    sp_send(b_row, B_SP + 16, origin[4])
    sp_forward(b_row, B_SP + 4, origin[1])
    sp_forward(b_row, B_SP + 8, origin[2])
    tm_got(b_tm, B_TM, 3)
    tm_step(b_tm, B_TM, 4)
    sp_send(b_row, B_SP + 20, origin[5])
    sp_send(b_row, B_SP + 24, origin[6])
    tm_got(row_a, A_TM, 1)
    tm_step(row_a, A_TM, 2)
    sp_forward(b_row, B_SP + 12, origin[3])
    sp_forward(b_row, B_SP + 16, origin[4])
    tm_got(b_tm, B_TM, 4)
    sp_send(b_row, B_SP + 28, origin[7])
    tm_got(row_a, A_TM, 2)
    tm_step(row_a, A_TM, 3)
    sp_forward(b_row, B_SP + 20, origin[5])
    sp_forward(b_row, B_SP + 24, origin[6])
    tm_got(row_a, A_TM, 3)
    tm_step(row_a, A_TM, 4)
    sp_forward(b_row, B_SP + 28, origin[7])

    for r in range(1, NTM):
        got(xbuf.at[behind(z, r, NTM)], L_TM + r)
    count = float(FR * TILES * CELLS * GS)
    zero = jnp.zeros((GS, CELLS), F32)

    def whole(v):
        return jnp.sum(jnp.sum(v, axis=1, keepdims=True), axis=0, keepdims=True)

    def total(i, acc):
        return acc + jnp.sum(xbuf[i].astype(F32), axis=0)

    mean = whole(lax.fori_loop(0, NTM, total, zero)) / count

    def spread(i, acc):
        v = xbuf[i].astype(F32) - mean
        return acc + jnp.sum(v * v, axis=0)

    inverse = lax.rsqrt(whole(lax.fori_loop(0, NTM, spread, zero)) / count + EPS)

    row16 = lax.broadcasted_iota(jnp.int32, (GS, CELLS), 0)
    lane16 = lax.broadcasted_iota(jnp.int32, (GS, CELLS), 1)
    diag = lane16 == z * GS + row16

    def column(ref):
        return jnp.sum(jnp.where(diag, ref[pl.ds(y, 1), :], 0.0), axis=1, keepdims=True)

    gamma, beta = column(gamma_ref), column(beta_ref)

    cell = lax.broadcasted_iota(jnp.int32, (8, GS, CELLS), 2)
    ix, iy = cell & (TW - 1), cell >> 4

    def inside(dy, dx):
        ok = None
        for cond in (
            [iy + dy >= 0] if dy < 0 else [iy + dy < TH] if dy > 0 else []
        ) + ([ix + dx >= 0] if dx < 0 else [ix + dx < TW] if dx > 0 else []):
            ok = cond if ok is None else ok & cond
        return ok

    def taps(i, _):
        normed = (xbuf[i].astype(F32) - mean) * inverse
        act = normed * gamma + beta
        sig = jax.nn.sigmoid(act)
        xh[i] = normed
        ds[i] = sig * (1.0 + act * (1.0 - sig))
        hidden = (act * sig).astype(BF16).astype(F32)
        base = pl.multiple_of((i + 1) * 1024, 1024)
        for s in range(9):
            dy, dx = s // 3 - 1, s % 3 - 1
            v = hidden
            if s != 4:
                v = pltpu.roll(v, (-(TW * dy + dx)) % CELLS, 2)
                v = jnp.where(inside(dy, dx), v, 0.0)
            v = v.astype(BF16)
            for j in range(8):
                a9[s * GS : (s + 1) * GS, pl.ds(base + j * CELLS, CELLS)] = v[j]
        return 0

    lax.fori_loop(0, NTM, taps, 0)
    a9[:, 0:512] = a9[:, 1024:1536]
    a9[:, 512:1024] = a9[:, 1024:1536]

    for i in range(8):
        got(wbuf.at[i], WGT + i)
    for i in range(8):
        wf[:, 2 * i : 2 * i + 2, :] = wbuf[i].astype(F32)
    for kt in range(3):
        wk[kt, 0:ROWS, :] = wf[9 * kt : 9 * kt + 9].reshape(ROWS, COUT).astype(BF16)
    pick_r = lax.broadcasted_iota(jnp.int32, (GS, COUT), 0)
    pick_o = lax.broadcasted_iota(jnp.int32, (GS, COUT), 1)
    wk[0, ROWS : ROWS + GS, :] = jnp.where(pick_o == mine * GS + pick_r, 1.0, 0.0).astype(BF16)

    for i in range(8):
        sp_got(b_row, B_SP + 4 * i, origin[i])
    tm_got(row_a, A_TM, 4)

    dk[...] = jnp.zeros_like(dk)

    def dweight(i, _):
        g = gz[pl.ds(2 + 2 * i, 2)].reshape(1024, COUT)
        for kt in range(3):
            a = a9[:, pl.ds(pl.multiple_of(1024 * i + 512 * kt, 512), 1024)]
            dk[9 * kt : 9 * kt + 9] += jnp.dot(a, g, preferred_element_type=F32).reshape(9, GS, COUT)
        return 0

    lax.fori_loop(0, NTM, dweight, 0)
    rscale = 1.0 / math.sqrt(NDP * FR * TILES * CELLS)
    for i in range(8):
        dsend[i] = dk[:, 2 * i : 2 * i + 2, :] * rscale
    for r in range(1, NDP):
        to = ahead(d, r, NDP)
        go(dsend.at[to], drecv.at[d], D_DP + r, {"dp": to})
    drecv[d] = dsend[d]

    nt = (((1,), (1,)), ((), ()))

    def back(e, _):
        sums = None
        for kt in range(3):
            g = gz[e + 2 - kt].reshape(512, COUT)
            w = wk[kt] if kt == 0 else wk[kt, 0:ROWS, :]
            v = lax.dot_general(w, g, nt, preferred_element_type=F32)
            if kt == 0:
                rest, sums = v[ROWS:], v[:ROWS]
            else:
                sums = sums + v
        for t in range(TILES):
            out = None
            for s in range(9):
                dy, dx = s // 3 - 1, s % 3 - 1
                v = sums[s * GS : (s + 1) * GS, t * CELLS : (t + 1) * CELLS]
                if s != 4:
                    v = pltpu.roll(v, (TW * dy + dx) % CELLS, 1)
                    v = jnp.where(inside(-dy, -dx)[0], v, 0.0)
                out = v if out is None else out + v
            dhb[TILES * e + t] = out
            rsd[TILES * e + t] = rest[:, t * CELLS : (t + 1) * CELLS]
        return 0

    lax.fori_loop(0, FR + 2, back, 0)
    dhb[8:12] = dhb[8:12] + (dhb[0:4] + dhb[4:8])

    def gains(i, acc):
        dact = dhb[pl.ds(8 + 8 * i, 8)] * ds[i]
        dhb[pl.ds(8 + 8 * i, 8)] = dact
        return acc[0] + jnp.sum(dact * xh[i], axis=0), acc[1] + jnp.sum(dact, axis=0)

    dgam, dbet = lax.fori_loop(0, NTM, gains, (zero, zero))
    dgam = jnp.sum(dgam, axis=1, keepdims=True)
    dbet = jnp.sum(dbet, axis=1, keepdims=True)
    m1 = jnp.sum(dbet * gamma, axis=0, keepdims=True) / count
    m2 = jnp.sum(dgam * gamma, axis=0, keepdims=True) / count

    gown[...] = jnp.zeros_like(gown)
    gown[0:1, :] = jnp.sum(jnp.where(diag, dgam * rscale, 0.0), axis=0, keepdims=True)
    gown[1:2, :] = jnp.sum(jnp.where(diag, dbet * rscale, 0.0), axis=0, keepdims=True)
    for r in range(1, NDP):
        to = ahead(d, r, NDP)
        go(gown, gdp.at[d], G_DP + r, {"dp": to})
    gdp[d] = gown[...]

    def dinput(i, _):
        v = inverse * (dhb[pl.ds(8 + 8 * i, 8)] * gamma - m1 - xh[i] * m2)
        dxs[i] = (v + rsd[pl.ds(8 * i, 8)]).astype(BF16)
        return 0

    lax.fori_loop(0, NTM, dinput, 0)
    for r in range(1, NTM):
        zo = ahead(z, r, NTM)
        go(dxs.at[zo], zback.at[z], D_TM + r, {"tm": zo})
    zback[z] = dxs[z]

    for r in range(1, NDP):
        got(drecv.at[behind(d, r, NDP)], D_DP + r)
    acc = drecv[0]
    for i in range(1, NDP):
        acc = acc + drecv[i]
    dsum[...] = acc
    to_owner = copy(dsum, dw_ref, D_OWN, src(d))

    @pl.when(self_t == 0)
    def _():
        to_owner.start()

    @pl.when(self_t == 1)
    def _():
        pltpu.make_async_copy(dsum, dw_ref, recv_sem.at[D_OWN]).start()

    for r in range(1, NDP):
        got(gdp.at[behind(d, r, NDP)], G_DP + r)
    acc = gdp[0]
    for i in range(1, NDP):
        acc = acc + gdp[i]
    gsum[...] = acc
    for r in range(NTM):
        for q in range(NSP):
            if r or q:
                to = {"tm": ahead(z, r, NTM), "space": ahead(y, q, NSP)}
                go(gsum, gall.at[z, y], G_ALL + r * NSP + q, to)
    gall[z, y] = gsum[...]

    for r in range(1, NTM):
        got(zback.at[behind(z, r, NTM)], D_TM + r)
    for t in range(TILES):
        for f in range(2):
            v = zback[:, f * TILES + t].astype(F32).reshape(NTM * GS, CELLS)
            tback[t, f] = v.T.astype(BF16)
    for yo in range(NSP):
        for j in range(CAP):
            tile, live = jnp.int32(0), jnp.int32(0)
            for t in range(TILES):
                here = (owners[t] == yo) & (ranks[t] == j)
                tile, live = jnp.where(here, t, tile), jnp.where(here, 1, live)
            v = tback[tile]
            ysend[yo, :, j] = jnp.where(live > 0, v, jnp.zeros_like(v))
    lanes = pl.ds(pl.multiple_of(y * 128, 128), 128)
    for r in range(1, NSP):
        yo = ahead(y, r, NSP)
        go(ysend.at[yo], dlat_ref.at[:, :, :, lanes], D_SP + r, {"space": yo})
    own = pltpu.make_async_copy(ysend.at[y], dlat_ref.at[:, :, :, lanes], own_sem.at[1])
    own.start()

    for r in range(NTM):
        for q in range(NSP):
            if r or q:
                got(gall.at[behind(z, r, NTM), behind(y, q, NSP)], G_ALL + r * NSP + q)
    for s in range(NSP):
        acc = gall[0, s]
        for i in range(1, NTM):
            acc = acc + gall[i, s]
        dgb_ref[:, s : s + 1, :] = acc[0:2].reshape(2, 1, 128)

    own.wait()
    for r in range(1, NSP):
        yo = behind(y, r, NSP)
        got(dlat_ref.at[:, :, :, pl.ds(pl.multiple_of(yo * 128, 128), 128)], D_SP + r)
    got(dw_ref, D_OWN)
    for c in started:
        c.wait_send()

    @pl.when(self_t == 0)
    def _():
        copy(dsum, dw_ref, D_OWN, src(d)).wait_send()

    @pl.when(jnp.logical_not(w_self))
    def _():
        copy(w_ref, wbuf.at[w_piece], WGT, {"tm": z}).wait_send()


def shards(latents, owner, gamma, beta, weight, upstream):
    vmem = pl.BlockSpec(memory_space=pltpu.VMEM)
    hbm = pl.BlockSpec(memory_space=pl.ANY)
    scratch = [
        ((FR + 4, TILES, CELLS, COUT), BF16),
        ((NSP, 2, CAP, CELLS, 128), BF16),
        ((NTM, 8, GS, CELLS), BF16),
        ((NTM, 8, GS, CELLS), BF16),
        ((8, TAPS, 2, COUT), BF16),
        ((TAPS, GS, COUT), F32),
        ((3, ROWS + GS, COUT), BF16),
        ((ROWS, 512 * (FR + 2)), BF16),
        ((NTM, 8, GS, CELLS), F32),
        ((NTM, 8, GS, CELLS), F32),
        ((TILES * (FR + 2), GS, CELLS), F32),
        ((TILES * (FR + 2), GS, CELLS), F32),
        ((TAPS, GS, COUT), F32),
        ((8, TAPS, 2, COUT), F32),
        ((8, TAPS, 2, COUT), F32),
        ((TAPS, 2, COUT), F32),
        ((NTM, 8, GS, CELLS), BF16),
        ((NTM, 8, GS, CELLS), BF16),
        ((TILES, 2, CELLS, 128), BF16),
        ((NSP, 2, CAP, CELLS, 128), BF16),
        ((8, 128), F32),
        ((NDP, 8, 128), F32),
        ((8, 128), F32),
        ((NTM, NSP, 8, 128), F32),
    ]
    dlat, dw, dgb = pl.pallas_call(
        body,
        out_shape=(
            jax.ShapeDtypeStruct((2, CAP, CELLS, C), BF16),
            jax.ShapeDtypeStruct((TAPS, 2, COUT), F32),
            jax.ShapeDtypeStruct((2, 4, 128), F32),
        ),
        in_specs=[pl.BlockSpec(memory_space=pltpu.SMEM), vmem, vmem, vmem, vmem, vmem],
        out_specs=(hbm, hbm, vmem),
        scratch_shapes=[pltpu.VMEM(s, t) for s, t in scratch]
        + [
            pltpu.SemaphoreType.DMA((N_SEM,)),
            pltpu.SemaphoreType.DMA((N_SEM,)),
            pltpu.SemaphoreType.DMA((2,)),
        ],
        compiler_params=pltpu.CompilerParams(
            collective_id=0, has_side_effects=True, vmem_limit_bytes=56 * 2**20
        ),
    )(
        owner,
        gamma.reshape(4, 128),
        beta.reshape(4, 128),
        latents[0],
        upstream.reshape(2, 4 * CELLS, COUT),
        weight.transpose(1, 0, 2),
    )
    return dlat[None], dw.transpose(1, 0, 2), dgb[0].reshape(C), dgb[1].reshape(C)


def solution(mesh):
    return jax.shard_map(
        shards,
        mesh=mesh,
        in_specs=(
            P("dp", "tm", "space", None, None),
            P("dp", None, None),
            P(),
            P(),
            P(("dp", "tm", "space"), None, None),
            P("dp", "tm", "space", None, None),
        ),
        out_specs=(
            P("dp", "tm", "space", None, None),
            P(("dp", "tm", "space"), None, None),
            P(),
            P(),
        ),
        check_vma=False,
    )
```

time: 786 us -> 95.7 us (0.12)
  the two profiles are of different devices: /device:TPU:1 before, /device:TPU:2 now
where the time goes in v1:
time: 95.7 us; the launch traced here: 95.5 us
  Pallas kernels  89.8 us (94%)
  local copies, waits for them, and re-layouts  5.07 us (5%)
    pallas_call x1, Pallas kernels, shards(): pl.pallas_call(body, out_shape=(jax.ShapeDtypeStruct((2, CAP, CELLS, C),...  89.8 us
    unnamed x9, local copies, waits for them, and re-layouts  4.49 us

profile of v1, /device:TPU:2, one launch (start us, length us, event | category | flops | bytes accessed | tf_op | source)
XLA Modules:
  0.0 95.5 jit_solution(11091815866383202067)
XLA Ops:
  0.6 0.0 copy-start.2
  0.6 0.6 copy-done.2
  1.3 0.7 copy.10.owner_ref
  1.9 89.8 %shard_map.93 = (bf16[2,2,128,512]{3,2,1,0:T(8,128)(2,1)}, f32[27,2,256]{2,1,0:T(2,128)}, f32[2,4,128]{2,1,0:T(4,128)}) custom-call(s32[1,4,1]{2,1,0:T(4,128)} %copy.10.owner_ref, f32[4,128]{1,0:T(4,128)} %bitcast.16, f32[4,128]{1,0:T(4,128)} %bitcast.17, bf16[2,2,128,512]{3,2,1,0:T(8,128)(2,1)} %bitcast.11, bf16[2,512,256]{2,1,0:T(8,128)(2,1)} %bitcast.12, ...), custom_call_target="tpu_custom_call" | custom-call | tf_op jit(solution)/shard_map/pallas_call | solution.py:498
  91.8 0.0 copy-start.1
  91.8 0.7 copy-done.1
  92.5 0.6 slice_bitcast_fusion
  93.0 0.0 copy-start
  93.0 1.9 %copy.13 = bf16[1,2,2,128,512]{4,3,2,1,0:T(8,128)(2,1)} copy(bf16[1,2,2,128,512]{4,3,2,1,0:T(8,128)(2,1)} %bitcast.13) | data formatting | bytes 1048576
  94.9 0.0 copy-done
  94.9 0.6 copy.14
Async XLA Ops:
  0.6 0.7 copy-start.2
  91.8 0.7 copy-start.1
  93.0 1.9 %copy-start = (f32[27,2,256]{2,1,0:T(2,128)S(1)}, f32[27,2,256]{2,1,0:T(2,128)}, u32[]{:S(2)}) copy-start(f32[27,2,256]{2,1,0:T(2,128)} %get-tuple-element.8) | copy-start | bytes 165892

commit v2 on v1

v2 whole, which is shorter than its diff:
```python
import math

import jax
import jax.numpy as jnp
from jax import lax
from jax.experimental import pallas as pl
from jax.experimental.pallas import tpu as pltpu
from jax.sharding import PartitionSpec as P

MESH = pl.DeviceIdType.MESH
F32 = jnp.float32
BF16 = jnp.bfloat16
EPS = 1e-06

NDP, NTM, NSP = 8, 8, 4
GROUPS = 32
GS = 16
FR = 16
TILES = 4
CAP = 2
TH, TW = 8, 16
CELLS = TH * TW
C, COUT = 512, 256
TAPS = 27
ROWS = 9 * GS
LEFT = 48

B_TM, B_SP, A_SP, A_TM = 0, 8, 40, 44
L_SP, L_TM, WGT = 76, 80, 88
D_TM, D_DP, G_DP, D_SP, D_OWN, G_ALL = 96, 112, 120, 128, 136, 137
N_SEM = 169


def body(
    owner_ref, gamma_ref, beta_ref, lat_ref, ups_ref, w_ref,
    dlat_ref, dw_ref, dgam_ref, dbet_ref,
    gz, ybuf, zsend, xbuf, wbuf, wf, wall, a9, xh, ds, dhb, rsd, dk, dsend, drecv, dsum,
    dxs, zback, tback, ysend, gown, gdp, gsum, gall, send_sem, recv_sem, own_sem,
):
    d, z, y = lax.axis_index("dp"), lax.axis_index("tm"), lax.axis_index("space")
    ahead = lambda v, r, n: lax.rem(v + r, n)
    behind = lambda v, r, n: lax.rem(v - r + n, n)
    line = (d * NTM + z) * NSP + y
    mine = y * NTM + z
    w_group = line // 8
    w_tm, w_sp = lax.rem(w_group, NTM), w_group // NTM
    w_piece = lax.rem(line, 8)
    src = lambda i: {
        "dp": mine // 4,
        "tm": 2 * lax.rem(mine, 4) + i // 4,
        "space": lax.rem(jnp.int32(i), 4) if not isinstance(i, int) else i % 4,
    }
    w_self = (w_tm == z) & (w_sp == y)
    own_piece_here = line // 8 == mine

    started = []

    def copy(a, b, n, to, m=None):
        return pltpu.make_async_remote_copy(
            src_ref=a, dst_ref=b, send_sem=send_sem.at[n], recv_sem=recv_sem.at[n if m is None else m],
            device_id=to, device_id_type=MESH,
        )

    def go(a, b, n, to, m=None):
        c = copy(a, b, n, to, m)
        c.start()
        started.append(c)
        return c

    def got(region, n):
        copy(region, region, n, {"tm": z}).wait_recv()

    barrier = pltpu.get_barrier_semaphore()

    def greet(to):
        pl.semaphore_signal(barrier, inc=1, device_id=to, device_id_type=MESH)

    for r in range(NTM):
        for q in range(NSP):
            if r or q:
                greet({"tm": ahead(z, r, NTM), "space": ahead(y, q, NSP)})
    for r in range(1, NDP):
        greet({"dp": ahead(d, r, NDP)})
    for i in range(8):
        o = src(i)

        @pl.when((8 * mine + i) != line)
        def _():
            greet(o)

    @pl.when(jnp.logical_not(own_piece_here & (w_piece == d)))
    def _():
        greet({"dp": w_piece, "tm": w_tm, "space": w_sp})

    p = lax.broadcasted_iota(jnp.int32, (CELLS, 4 * CELLS), 0)
    q = lax.broadcasted_iota(jnp.int32, (CELLS, 4 * CELLS), 1)
    pool = ((q >> 6) == (p >> 4)) & (((q & 31) >> 1) == (p & 15))
    pool = jnp.where(pool, 1.0, 0.0).astype(BF16)
    for f in range(2):
        pooled = jnp.dot(pool, ups_ref[f], preferred_element_type=F32)
        gz[2 * z + f, y] = pooled.astype(BF16)
    dhb[...] = jnp.zeros_like(dhb)
    dk[...] = jnp.zeros_like(dk)

    self_w = jnp.where(w_self, 1, 0)
    self_o = jnp.where(own_piece_here & (w_piece == d), 1, 0)
    self_s = jnp.where(own_piece_here, 1, 0)
    own_to = 8 * mine + d
    self_t = jnp.where(own_to == line, 1, 0)
    pl.semaphore_wait(barrier, NTM * NSP - 1 + NDP - 1 + 8 - self_s + 1 - self_t)

    def part_b(zo, yo, f=0, n=2):
        return gz.at[pl.ds(2 * zo + f, n), yo, pl.ds(LEFT, CELLS - LEFT)]

    def part_a(zo, yo, f=0, n=2):
        return gz.at[pl.ds(2 * zo + f, n), yo, pl.ds(0, LEFT)]

    zr, zl = {"tm": ahead(z, 1, NTM)}, {"tm": behind(z, 1, NTM)}
    yr, yl = {"space": ahead(y, 1, NSP)}, {"space": behind(y, 1, NSP)}
    yo_r, yo_l, yo_2 = ahead(y, 1, NSP), behind(y, 1, NSP), ahead(y, 2, NSP)

    def tm_step(region, base, h):
        frames = (dict(f=0, n=2),) * 2 if h < 4 else (dict(f=0, n=1), dict(f=1, n=1))
        for way, (to, o) in enumerate(((zr, behind(z, h - 1, NTM)), (zl, ahead(z, h - 1, NTM)))):
            a = region(o, **frames[way])
            go(a, a, base + 2 * (h - 1) + way, to)

    def tm_got(region, base, h):
        frames = (dict(f=0, n=2),) * 2 if h < 4 else (dict(f=0, n=1), dict(f=1, n=1))
        for way, o in enumerate((behind(z, h, NTM), ahead(z, h, NTM))):
            got(region(o, **frames[way]), base + 2 * (h - 1) + way)

    def sp_send(region, base, zo):
        a = region(zo, y)
        go(a, a, base, yr)
        go(a, a, base + 1, yl)

    def sp_forward(region, base, zo):
        got(region(zo, yo_l), base)
        a = region(zo, yo_l, 0, 1)
        go(a, a, base + 2, yr)
        got(region(zo, yo_r), base + 1)
        a = region(zo, yo_r, 1, 1)
        go(a, a, base + 3, yl)

    def sp_got(region, base, zo):
        got(region(zo, yo_2, 0, 1), base + 2)
        got(region(zo, yo_2, 1, 1), base + 3)

    steps = (0, -1, 1, -2, 2, -3, 3, 4)
    origin = [lax.rem(z + s + NTM, NTM) for s in steps]
    b_row = lambda zo, yo, f=0, n=2: part_b(zo, yo, f, n)
    b_tm = lambda zo, f=0, n=2: part_b(zo, y, f, n)

    sides = (y, yo_l, yo_r, yo_2)
    a_tm = [lambda zo, f=0, n=2, yo=yo: part_a(zo, yo, f, n) for yo in sides]
    near = [(0,), (1, 2), (3, 4), (5, 6), (7,)]

    def wave(h):
        tm_got(b_tm, B_TM, h)
        if h < 4:
            tm_step(b_tm, B_TM, h + 1)
        for b in near[h]:
            sp_send(b_row, B_SP + 4 * b, origin[b])
        for q in range(4):
            tm_got(a_tm[q], A_TM + 8 * q, h)
            if h < 4:
                tm_step(a_tm[q], A_TM + 8 * q, h + 1)

    def forward(h):
        for b in near[h]:
            sp_forward(b_row, B_SP + 4 * b, origin[b])

    def complete(h):
        for b in near[h]:
            sp_got(b_row, B_SP + 4 * b, origin[b])

    def block(h, i):
        return lax.rem(z + (2 * i - 1) * h + NTM, NTM)

    sp_send(part_a, A_SP, z)
    tm_step(b_tm, B_TM, 1)
    tm_step(a_tm[0], A_TM, 1)
    sp_send(b_row, B_SP, z)

    for r in range(NDP):
        to = {"dp": ahead(d, r, NDP), "tm": w_tm, "space": w_sp}
        c = copy(w_ref, wbuf.at[w_piece], WGT + r, to, WGT + w_piece)
        if r:
            c.start()
            started.append(c)
        else:

            @pl.when(jnp.logical_not(w_self))
            def _():
                c.start()

            @pl.when(w_self)
            def _():
                pltpu.make_async_copy(w_ref, wbuf.at[w_piece], recv_sem.at[WGT + w_piece]).start()

    sp_forward(part_a, A_SP, z)
    tm_step(a_tm[1], A_TM + 8, 1)
    tm_step(a_tm[2], A_TM + 16, 1)

    for r in range(1, NSP):
        yo = ahead(y, r, NSP)
        go(
            lat_ref.at[:, :, :, pl.ds(pl.multiple_of(yo * 128, 128), 128)],
            ybuf.at[y], L_SP + r, {"space": yo},
        )
    own = pltpu.make_async_copy(
        lat_ref.at[:, :, :, pl.ds(pl.multiple_of(y * 128, 128), 128)], ybuf.at[y], own_sem.at[0]
    )
    own.start()

    sp_got(part_a, A_SP, z)
    tm_step(a_tm[3], A_TM + 24, 1)
    wave(1)
    forward(0)

    own.wait()
    for r in range(1, NSP):
        got(ybuf.at[behind(y, r, NSP)], L_SP + r)
    owners = [owner_ref[t] for t in range(TILES)]
    ranks = [
        jnp.minimum(
            sum([(owners[u] == owners[t]).astype(jnp.int32) for u in range(t)], jnp.int32(0)), CAP - 1
        )
        for t in range(TILES)
    ]
    for t in range(TILES):
        for f in range(2):
            v = ybuf[owners[t], f, ranks[t]].astype(F32)
            zsend[:, f * TILES + t] = v.T.reshape(NTM, GS, CELLS).astype(BF16)
    for r in range(1, NTM):
        zo = ahead(z, r, NTM)
        go(zsend.at[zo], xbuf.at[z], L_TM + r, {"tm": zo})
    xbuf[z] = zsend[z]

    for i in range(8):
        got(wbuf.at[i], WGT + i)
    for i in range(8):
        wf[:, 2 * i : 2 * i + 2, :] = wbuf[i].astype(F32)
    wall[0 : 3 * ROWS, :] = wf[...].reshape(3 * ROWS, COUT).astype(BF16)
    pick_r = lax.broadcasted_iota(jnp.int32, (GS, COUT), 0)
    pick_o = lax.broadcasted_iota(jnp.int32, (GS, COUT), 1)
    wall[3 * ROWS : 3 * ROWS + GS, :] = jnp.where(pick_o == mine * GS + pick_r, 1.0, 0.0).astype(BF16)

    cell = lax.broadcasted_iota(jnp.int32, (8, GS, CELLS), 2)
    ix, iy = cell & (TW - 1), cell >> 4

    def inside(dy, dx):
        ok = None
        for cond in (
            [iy + dy >= 0] if dy < 0 else [iy + dy < TH] if dy > 0 else []
        ) + ([ix + dx >= 0] if dx < 0 else [ix + dx < TW] if dx > 0 else []):
            ok = cond if ok is None else ok & cond
        return ok

    nt = (((1,), (1,)), ((), ()))

    def dhidden(h):
        def frame(n, _):
            f = 2 * block(h, n // 2) + lax.rem(n, 2)
            v = lax.dot_general(
                wall[...], gz[f].reshape(TILES * CELLS, COUT), nt, preferred_element_type=F32
            )
            for t in range(TILES):
                lanes = slice(t * CELLS, (t + 1) * CELLS)
                rsd[TILES * f + t] = v[3 * ROWS :, lanes]
                for kt in range(3):
                    out = None
                    for s in range(9):
                        dy, dx = s // 3 - 1, s % 3 - 1
                        w = v[kt * ROWS + s * GS : kt * ROWS + (s + 1) * GS, lanes]
                        if s != 4:
                            w = pltpu.roll(w, (TW * dy + dx) % CELLS, 1)
                            w = jnp.where(inside(-dy, -dx)[0], w, 0.0)
                        out = w if out is None else out + w
                    dhb[TILES * (f + kt) + t] += out
            return 0

        lax.fori_loop(0, 2 * len(near[h]), frame, 0)

    def dweight(h):
        def one(n, _):
            i = block(h, n)
            g = gz[pl.ds(2 * i, 2)].reshape(1024, COUT)
            for kt in range(3):
                a = a9[:, pl.ds(pl.multiple_of(1024 * i + 512 * kt, 512), 1024)]
                dk[9 * kt : 9 * kt + 9] += jnp.dot(a, g, preferred_element_type=F32).reshape(9, GS, COUT)
            return 0

        lax.fori_loop(0, len(near[h]), one, 0)

    wave(2)
    forward(1)
    complete(0)
    dhidden(0)

    wave(3)
    forward(2)

    for r in range(1, NTM):
        got(xbuf.at[behind(z, r, NTM)], L_TM + r)
    count = float(FR * TILES * CELLS * GS)
    zero = jnp.zeros((GS, CELLS), F32)

    def whole(v):
        return jnp.sum(jnp.sum(v, axis=1, keepdims=True), axis=0, keepdims=True)

    def total(i, acc):
        return acc + jnp.sum(xbuf[i].astype(F32), axis=0)

    mean = whole(lax.fori_loop(0, NTM, total, zero)) / count

    def spread(i, acc):
        v = xbuf[i].astype(F32) - mean
        return acc + jnp.sum(v * v, axis=0)

    inverse = lax.rsqrt(whole(lax.fori_loop(0, NTM, spread, zero)) / count + EPS)

    row16 = lax.broadcasted_iota(jnp.int32, (GS, CELLS), 0)
    lane16 = lax.broadcasted_iota(jnp.int32, (GS, CELLS), 1)
    diag = lane16 == z * GS + row16

    def column(ref):
        return jnp.sum(jnp.where(diag, ref[pl.ds(y, 1), :], 0.0), axis=1, keepdims=True)

    gamma, beta = column(gamma_ref), column(beta_ref)

    def taps(i, _):
        normed = (xbuf[i].astype(F32) - mean) * inverse
        act = normed * gamma + beta
        sig = jax.nn.sigmoid(act)
        xh[i] = normed
        ds[i] = sig * (1.0 + act * (1.0 - sig))
        hidden = (act * sig).astype(BF16).astype(F32)
        base = pl.multiple_of((i + 1) * 1024, 1024)
        for s in range(9):
            dy, dx = s // 3 - 1, s % 3 - 1
            v = hidden
            if s != 4:
                v = pltpu.roll(v, (-(TW * dy + dx)) % CELLS, 2)
                v = jnp.where(inside(dy, dx), v, 0.0)
            v = v.astype(BF16)
            for j in range(8):
                a9[s * GS : (s + 1) * GS, pl.ds(base + j * CELLS, CELLS)] = v[j]
        return 0

    lax.fori_loop(0, NTM, taps, 0)
    a9[:, 0:512] = a9[:, 1024:1536]
    a9[:, 512:1024] = a9[:, 1024:1536]

    complete(1)
    dhidden(1)

    wave(4)
    forward(3)
    complete(2)
    dhidden(2)
    forward(4)
    dweight(0)
    dweight(1)
    dweight(2)
    complete(3)
    dhidden(3)
    dweight(3)
    complete(4)
    dweight(4)

    rscale = 1.0 / math.sqrt(NDP * FR * TILES * CELLS)
    for i in range(8):
        dsend[i] = dk[:, 2 * i : 2 * i + 2, :] * rscale
    for r in range(1, NDP):
        to = ahead(d, r, NDP)
        go(dsend.at[to], drecv.at[d], D_DP + r, {"dp": to})
    drecv[d] = dsend[d]

    dhidden(4)
    dhb[8:12] = dhb[8:12] + (dhb[0:4] + dhb[4:8])

    def gains(i, acc):
        dact = dhb[pl.ds(8 + 8 * i, 8)] * ds[i]
        dhb[pl.ds(8 + 8 * i, 8)] = dact
        return acc[0] + jnp.sum(dact * xh[i], axis=0), acc[1] + jnp.sum(dact, axis=0)

    dgam, dbet = lax.fori_loop(0, NTM, gains, (zero, zero))
    dgam = jnp.sum(dgam, axis=1, keepdims=True)
    dbet = jnp.sum(dbet, axis=1, keepdims=True)
    m1 = jnp.sum(dbet * gamma, axis=0, keepdims=True) / count
    m2 = jnp.sum(dgam * gamma, axis=0, keepdims=True) / count

    def dinput(i, _):
        v = inverse * (dhb[pl.ds(8 + 8 * i, 8)] * gamma - m1 - xh[i] * m2)
        dxs[i] = (v + rsd[pl.ds(8 * i, 8)]).astype(BF16)
        return 0

    lax.fori_loop(0, NTM, dinput, 0)

    def of_frame(ref, i, f):
        return ref.at[i, pl.ds(f * TILES, TILES)]

    for f in range(2):
        for r in range(1, NTM):
            zo = ahead(z, r, NTM)
            go(of_frame(dxs, zo, f), of_frame(zback, z, f), D_TM + 8 * f + r, {"tm": zo})
    zback[z] = dxs[z]

    gown[...] = jnp.zeros_like(gown)
    gown[0:1, :] = jnp.sum(jnp.where(diag, dgam * rscale, 0.0), axis=0, keepdims=True)
    gown[1:2, :] = jnp.sum(jnp.where(diag, dbet * rscale, 0.0), axis=0, keepdims=True)
    for r in range(1, NDP):
        to = ahead(d, r, NDP)
        go(gown, gdp.at[d], G_DP + r, {"dp": to})
    gdp[d] = gown[...]

    lanes = pl.ds(pl.multiple_of(y * 128, 128), 128)

    def to_slots(f):
        for r in range(1, NTM):
            got(of_frame(zback, behind(z, r, NTM), f), D_TM + 8 * f + r)
        for t in range(TILES):
            v = zback[:, f * TILES + t].astype(F32).reshape(NTM * GS, CELLS)
            tback[f, t] = v.T.astype(BF16)
        for yo in range(NSP):
            for j in range(CAP):
                tile, live = jnp.int32(0), jnp.int32(0)
                for t in range(TILES):
                    here = (owners[t] == yo) & (ranks[t] == j)
                    tile, live = jnp.where(here, t, tile), jnp.where(here, 1, live)
                v = tback[f, tile]
                ysend[f, yo, j] = jnp.where(live > 0, v, jnp.zeros_like(v))
        for r in range(1, NSP):
            yo = ahead(y, r, NSP)
            go(ysend.at[f, yo], dlat_ref.at[f, :, :, lanes], D_SP + 4 * f + r, {"space": yo})
        own = pltpu.make_async_copy(ysend.at[f, y], dlat_ref.at[f, :, :, lanes], own_sem.at[1 + f])
        own.start()
        return own

    owns = [to_slots(0)]

    for r in range(1, NDP):
        got(gdp.at[behind(d, r, NDP)], G_DP + r)
    acc = gdp[0]
    for i in range(1, NDP):
        acc = acc + gdp[i]
    gsum[...] = acc
    for r in range(NTM):
        for q in range(NSP):
            if r or q:
                to = {"tm": ahead(z, r, NTM), "space": ahead(y, q, NSP)}
                go(gsum, gall.at[z, y], G_ALL + r * NSP + q, to)
    gall[z, y] = gsum[...]

    owns.append(to_slots(1))

    for r in range(1, NDP):
        got(drecv.at[behind(d, r, NDP)], D_DP + r)
    acc = drecv[0]
    for i in range(1, NDP):
        acc = acc + drecv[i]
    dsum[...] = acc
    to_owner = copy(dsum, dw_ref, D_OWN, src(d))

    @pl.when(self_t == 0)
    def _():
        to_owner.start()

    @pl.when(self_t == 1)
    def _():
        pltpu.make_async_copy(dsum, dw_ref, recv_sem.at[D_OWN]).start()

    for r in range(NTM):
        for q in range(NSP):
            if r or q:
                got(gall.at[behind(z, r, NTM), behind(y, q, NSP)], G_ALL + r * NSP + q)
    for s in range(NSP):
        acc = gall[0, s]
        for i in range(1, NTM):
            acc = acc + gall[i, s]
        dgam_ref[s : s + 1, :] = acc[0:1]
        dbet_ref[s : s + 1, :] = acc[1:2]

    for f in range(2):
        owns[f].wait()
        for r in range(1, NSP):
            yo = behind(y, r, NSP)
            got(dlat_ref.at[f, :, :, pl.ds(pl.multiple_of(yo * 128, 128), 128)], D_SP + 4 * f + r)
    got(dw_ref, D_OWN)
    for c in started:
        c.wait_send()

    @pl.when(self_t == 0)
    def _():
        copy(dsum, dw_ref, D_OWN, src(d)).wait_send()

    @pl.when(jnp.logical_not(w_self))
    def _():
        copy(w_ref, wbuf.at[w_piece], WGT, {"tm": z}).wait_send()


def shards(latents, owner, gamma, beta, weight, upstream):
    vmem = pl.BlockSpec(memory_space=pltpu.VMEM)
    hbm = pl.BlockSpec(memory_space=pl.ANY)
    scratch = [
        ((FR, TILES, CELLS, COUT), BF16),
        ((NSP, 2, CAP, CELLS, 128), BF16),
        ((NTM, 8, GS, CELLS), BF16),
        ((NTM, 8, GS, CELLS), BF16),
        ((8, TAPS, 2, COUT), BF16),
        ((TAPS, GS, COUT), F32),
        ((3 * ROWS + GS, COUT), BF16),
        ((ROWS, 512 * (FR + 2)), BF16),
        ((NTM, 8, GS, CELLS), F32),
        ((NTM, 8, GS, CELLS), F32),
        ((TILES * (FR + 2), GS, CELLS), F32),
        ((TILES * FR, GS, CELLS), F32),
        ((TAPS, GS, COUT), F32),
        ((8, TAPS, 2, COUT), F32),
        ((8, TAPS, 2, COUT), F32),
        ((TAPS, 2, COUT), F32),
        ((NTM, 8, GS, CELLS), BF16),
        ((NTM, 8, GS, CELLS), BF16),
        ((2, TILES, CELLS, 128), BF16),
        ((2, NSP, CAP, CELLS, 128), BF16),
        ((8, 128), F32),
        ((NDP, 8, 128), F32),
        ((8, 128), F32),
        ((NTM, NSP, 8, 128), F32),
    ]
    dlat, dw, dgam, dbet = pl.pallas_call(
        body,
        out_shape=(
            jax.ShapeDtypeStruct((2, CAP, CELLS, C), BF16),
            jax.ShapeDtypeStruct((TAPS, 2, COUT), F32),
            jax.ShapeDtypeStruct((4, 128), F32),
            jax.ShapeDtypeStruct((4, 128), F32),
        ),
        in_specs=[pl.BlockSpec(memory_space=pltpu.SMEM), vmem, vmem, vmem, vmem, vmem],
        out_specs=(hbm, hbm, vmem, vmem),
        scratch_shapes=[pltpu.VMEM(s, t) for s, t in scratch]
        + [
            pltpu.SemaphoreType.DMA((N_SEM,)),
            pltpu.SemaphoreType.DMA((N_SEM,)),
            pltpu.SemaphoreType.DMA((3,)),
        ],
        compiler_params=pltpu.CompilerParams(
            collective_id=0, has_side_effects=True, vmem_limit_bytes=56 * 2**20
        ),
    )(
        owner.reshape(TILES),
        gamma.reshape(4, 128),
        beta.reshape(4, 128),
        latents[0],
        upstream.reshape(2, 4 * CELLS, COUT),
        weight.transpose(1, 0, 2),
    )
    return dlat[None], dw.transpose(1, 0, 2), dgam.reshape(C), dbet.reshape(C)


def solution(mesh):
    return jax.shard_map(
        shards,
        mesh=mesh,
        in_specs=(
            P("dp", "tm", "space", None, None),
            P("dp", None, None),
            P(),
            P(),
            P(("dp", "tm", "space"), None, None),
            P("dp", "tm", "space", None, None),
        ),
        out_specs=(
            P("dp", "tm", "space", None, None),
            P(("dp", "tm", "space"), None, None),
            P(),
            P(),
        ),
        check_vma=False,
    )
```

time: 95.7 us -> 89.5 us (0.935)
  the two profiles are of different devices: /device:TPU:2 before, /device:TPU:1 now
where the time goes in v2:
time: 89.5 us; the launch traced here: 88.3 us
  Pallas kernels  83.9 us (94%)
  local copies, waits for them, and re-layouts  3.77 us (4%)
    pallas_call x1, Pallas kernels, shards(): pl.pallas_call(body, out_shape=(jax.ShapeDtypeStruct((2, CAP, CELLS, C),...  83.9 us
    unnamed x10, local copies, waits for them, and re-layouts  3.77 us

profile of v2, /device:TPU:1, one launch (start us, length us, event | category | flops | bytes accessed | tf_op | source)
XLA Modules:
  0.0 88.3 jit_solution(14449115918994351826)
XLA Ops:
  0.6 83.9 %shard_map.93 = (bf16[2,2,128,512]{3,2,1,0:T(8,128)(2,1)}, f32[27,2,256]{2,1,0:T(2,128)}, f32[4,128]{1,0:T(4,128)}, f32[4,128]{1,0:T(4,128)}) custom-call(s32[4]{0:T(128)} %bitcast.19, f32[4,128]{1,0:T(4,128)} %bitcast.15, f32[4,128]{1,0:T(4,128)} %bitcast.16, bf16[2,2,128,512]{3,2,1,0:T(8,128)(2,1)} %bitcast.10, bf16[2,512,256]{2,1,0:T(8,128)(2,1)} %bitcast.11, ...), custom_call_target="tpu_custom_call" | custom-call | tf_op jit(solution)/shard_map/pallas_call | solution.py:533
  84.5 0.0 copy-start
  84.5 1.9 %copy.14 = bf16[1,2,2,128,512]{4,3,2,1,0:T(8,128)(2,1)} copy(bf16[1,2,2,128,512]{4,3,2,1,0:T(8,128)(2,1)} %bitcast.12) | data formatting | bytes 1048576
  86.4 0.0 copy-done
  86.4 0.0 copy-start.2
  86.4 0.6 copy.15
  87.0 0.0 copy-done.2
  87.0 0.0 copy-start.1
  87.0 0.6 copy.16
  87.6 0.1 copy-done.1
  87.7 0.6 copy.17
Async XLA Ops:
  84.5 1.9 %copy-start = (f32[27,2,256]{2,1,0:T(2,128)S(1)}, f32[27,2,256]{2,1,0:T(2,128)}, u32[]{:S(2)}) copy-start(f32[27,2,256]{2,1,0:T(2,128)} %get-tuple-element.9) | copy-start | bytes 165892
  86.4 0.6 copy-start.2
  87.0 0.7 copy-start.1

commit v3 on v2

--- a/solution.py
+++ b/solution.py
@@ -27,8 +27,8 @@
 
 B_TM, B_SP, A_SP, A_TM = 0, 8, 40, 44
 L_SP, L_TM, WGT = 76, 80, 88
-D_TM, D_DP, G_DP, D_SP, D_OWN, G_ALL = 96, 112, 120, 128, 136, 137
-N_SEM = 169
+D_TM, D_DP, G_DP, D_SP, D_OWN, G_ALL = 112, 128, 136, 144, 152, 153
+N_SEM = 185
 
 
 def body(
@@ -51,6 +51,7 @@
         "space": lax.rem(jnp.int32(i), 4) if not isinstance(i, int) else i % 4,
     }
     w_self = (w_tm == z) & (w_sp == y)
+    w_home = d == mine // 4
     own_piece_here = line // 8 == mine
 
     started = []
@@ -81,13 +82,6 @@
                 greet({"tm": ahead(z, r, NTM), "space": ahead(y, q, NSP)})
     for r in range(1, NDP):
         greet({"dp": ahead(d, r, NDP)})
-    for i in range(8):
-        o = src(i)
-
-        @pl.when((8 * mine + i) != line)
-        def _():
-            greet(o)
-
     @pl.when(jnp.logical_not(own_piece_here & (w_piece == d)))
     def _():
         greet({"dp": w_piece, "tm": w_tm, "space": w_sp})
@@ -102,12 +96,9 @@
     dhb[...] = jnp.zeros_like(dhb)
     dk[...] = jnp.zeros_like(dk)
 
-    self_w = jnp.where(w_self, 1, 0)
-    self_o = jnp.where(own_piece_here & (w_piece == d), 1, 0)
-    self_s = jnp.where(own_piece_here, 1, 0)
     own_to = 8 * mine + d
     self_t = jnp.where(own_to == line, 1, 0)
-    pl.semaphore_wait(barrier, NTM * NSP - 1 + NDP - 1 + 8 - self_s + 1 - self_t)
+    pl.semaphore_wait(barrier, NTM * NSP - 1 + NDP - 1 + 1 - self_t)
 
     def part_b(zo, yo, f=0, n=2):
         return gz.at[pl.ds(2 * zo + f, n), yo, pl.ds(LEFT, CELLS - LEFT)]
@@ -156,12 +147,14 @@
     a_tm = [lambda zo, f=0, n=2, yo=yo: part_a(zo, yo, f, n) for yo in sides]
     near = [(0,), (1, 2), (3, 4), (5, 6), (7,)]
 
-    def wave(h):
+    def wave_b(h):
         tm_got(b_tm, B_TM, h)
         if h < 4:
             tm_step(b_tm, B_TM, h + 1)
         for b in near[h]:
             sp_send(b_row, B_SP + 4 * b, origin[b])
+
+    def wave_a(h):
         for q in range(4):
             tm_got(a_tm[q], A_TM + 8 * q, h)
             if h < 4:
@@ -177,75 +170,6 @@
 
     def block(h, i):
         return lax.rem(z + (2 * i - 1) * h + NTM, NTM)
-
-    sp_send(part_a, A_SP, z)
-    tm_step(b_tm, B_TM, 1)
-    tm_step(a_tm[0], A_TM, 1)
-    sp_send(b_row, B_SP, z)
-
-    for r in range(NDP):
-        to = {"dp": ahead(d, r, NDP), "tm": w_tm, "space": w_sp}
-        c = copy(w_ref, wbuf.at[w_piece], WGT + r, to, WGT + w_piece)
-        if r:
-            c.start()
-            started.append(c)
-        else:
-
-            @pl.when(jnp.logical_not(w_self))
-            def _():
-                c.start()
-
-            @pl.when(w_self)
-            def _():
-                pltpu.make_async_copy(w_ref, wbuf.at[w_piece], recv_sem.at[WGT + w_piece]).start()
-
-    sp_forward(part_a, A_SP, z)
-    tm_step(a_tm[1], A_TM + 8, 1)
-    tm_step(a_tm[2], A_TM + 16, 1)
-
-    for r in range(1, NSP):
-        yo = ahead(y, r, NSP)
-        go(
-            lat_ref.at[:, :, :, pl.ds(pl.multiple_of(yo * 128, 128), 128)],
-            ybuf.at[y], L_SP + r, {"space": yo},
-        )
-    own = pltpu.make_async_copy(
-        lat_ref.at[:, :, :, pl.ds(pl.multiple_of(y * 128, 128), 128)], ybuf.at[y], own_sem.at[0]
-    )
-    own.start()
-
-    sp_got(part_a, A_SP, z)
-    tm_step(a_tm[3], A_TM + 24, 1)
-    wave(1)
-    forward(0)
-
-    own.wait()
-    for r in range(1, NSP):
-        got(ybuf.at[behind(y, r, NSP)], L_SP + r)
-    owners = [owner_ref[t] for t in range(TILES)]
-    ranks = [
-        jnp.minimum(
-            sum([(owners[u] == owners[t]).astype(jnp.int32) for u in range(t)], jnp.int32(0)), CAP - 1
-        )
-        for t in range(TILES)
-    ]
-    for t in range(TILES):
-        for f in range(2):
-            v = ybuf[owners[t], f, ranks[t]].astype(F32)
-            zsend[:, f * TILES + t] = v.T.reshape(NTM, GS, CELLS).astype(BF16)
-    for r in range(1, NTM):
-        zo = ahead(z, r, NTM)
-        go(zsend.at[zo], xbuf.at[z], L_TM + r, {"tm": zo})
-    xbuf[z] = zsend[z]
-
-    for i in range(8):
-        got(wbuf.at[i], WGT + i)
-    for i in range(8):
-        wf[:, 2 * i : 2 * i + 2, :] = wbuf[i].astype(F32)
-    wall[0 : 3 * ROWS, :] = wf[...].reshape(3 * ROWS, COUT).astype(BF16)
-    pick_r = lax.broadcasted_iota(jnp.int32, (GS, COUT), 0)
-    pick_o = lax.broadcasted_iota(jnp.int32, (GS, COUT), 1)
-    wall[3 * ROWS : 3 * ROWS + GS, :] = jnp.where(pick_o == mine * GS + pick_r, 1.0, 0.0).astype(BF16)
 
     cell = lax.broadcasted_iota(jnp.int32, (8, GS, CELLS), 2)
     ix, iy = cell & (TW - 1), cell >> 4
@@ -294,13 +218,89 @@
 
         lax.fori_loop(0, len(near[h]), one, 0)
 
-    wave(2)
+    sp_send(part_a, A_SP, z)
+    tm_step(b_tm, B_TM, 1)
+    sp_send(b_row, B_SP, z)
+
+    to_group = copy(w_ref, wbuf.at[w_piece], WGT + 8, {"tm": w_tm, "space": w_sp}, WGT + w_piece)
+
+    @pl.when(jnp.logical_not(w_self))
+    def _():
+        to_group.start()
+
+    @pl.when(w_self)
+    def _():
+        pltpu.make_async_copy(w_ref, wbuf.at[w_piece], recv_sem.at[WGT + w_piece]).start()
+
+    wave_b(1)
+    sp_forward(part_a, A_SP, z)
+    for q in range(3):
+        tm_step(a_tm[q], A_TM + 8 * q, 1)
+    wave_b(2)
+
+    for r in range(1, NSP):
+        yo = ahead(y, r, NSP)
+        go(
+            lat_ref.at[:, :, :, pl.ds(pl.multiple_of(yo * 128, 128), 128)],
+            ybuf.at[y], L_SP + r, {"space": yo},
+        )
+    own = pltpu.make_async_copy(
+        lat_ref.at[:, :, :, pl.ds(pl.multiple_of(y * 128, 128), 128)], ybuf.at[y], own_sem.at[0]
+    )
+    own.start()
+
+    sp_got(part_a, A_SP, z)
+    tm_step(a_tm[3], A_TM + 24, 1)
+    forward(0)
+
+    @pl.when(w_home)
+    def _():
+        for i in range(8):
+            got(wbuf.at[i], WGT + i)
+        for r in range(1, NDP):
+            copy(wbuf, wbuf, WGT + 9 + r, {"dp": ahead(d, r, NDP)}, WGT + 9).start()
+
+    wave_b(3)
+    wave_a(1)
+    wave_b(4)
+
+    own.wait()
+    for r in range(1, NSP):
+        got(ybuf.at[behind(y, r, NSP)], L_SP + r)
+    owners = [owner_ref[t] for t in range(TILES)]
+    ranks = [
+        jnp.minimum(
+            sum([(owners[u] == owners[t]).astype(jnp.int32) for u in range(t)], jnp.int32(0)), CAP - 1
+        )
+        for t in range(TILES)
+    ]
+    for t in range(TILES):
+        for f in range(2):
+            v = ybuf[owners[t], f, ranks[t]].astype(F32)
+            zsend[:, f * TILES + t] = v.T.reshape(NTM, GS, CELLS).astype(BF16)
+    for r in range(1, NTM):
+        zo = ahead(z, r, NTM)
+        go(zsend.at[zo], xbuf.at[z], L_TM + r, {"tm": zo})
+    xbuf[z] = zsend[z]
+
+    @pl.when(jnp.logical_not(w_home))
+    def _():
+        got(wbuf, WGT + 9)
+
+    for i in range(8):
+        wf[:, 2 * i : 2 * i + 2, :] = wbuf[i].astype(F32)
+    wall[0 : 3 * ROWS, :] = wf[...].reshape(3 * ROWS, COUT).astype(BF16)
+    pick_r = lax.broadcasted_iota(jnp.int32, (GS, COUT), 0)
+    pick_o = lax.broadcasted_iota(jnp.int32, (GS, COUT), 1)
+    wall[3 * ROWS : 3 * ROWS + GS, :] = jnp.where(pick_o == mine * GS + pick_r, 1.0, 0.0).astype(BF16)
+
     forward(1)
     complete(0)
     dhidden(0)
-
-    wave(3)
+    wave_a(2)
     forward(2)
+    complete(1)
+    dhidden(1)
 
     for r in range(1, NTM):
         got(xbuf.at[behind(z, r, NTM)], L_TM + r)
@@ -353,20 +353,18 @@
     a9[:, 0:512] = a9[:, 1024:1536]
     a9[:, 512:1024] = a9[:, 1024:1536]
 
-    complete(1)
-    dhidden(1)
-
-    wave(4)
+    wave_a(3)
     forward(3)
+    dweight(0)
+    dweight(1)
     complete(2)
     dhidden(2)
+    dweight(2)
     forward(4)
-    dweight(0)
-    dweight(1)
-    dweight(2)
     complete(3)
     dhidden(3)
     dweight(3)
+    wave_a(4)
     complete(4)
     dweight(4)
 
@@ -408,7 +406,6 @@
             go(of_frame(dxs, zo, f), of_frame(zback, z, f), D_TM + 8 * f + r, {"tm": zo})
     zback[z] = dxs[z]
 
-    gown[...] = jnp.zeros_like(gown)
     gown[0:1, :] = jnp.sum(jnp.where(diag, dgam * rscale, 0.0), axis=0, keepdims=True)
     gown[1:2, :] = jnp.sum(jnp.where(diag, dbet * rscale, 0.0), axis=0, keepdims=True)
     for r in range(1, NDP):
@@ -498,7 +495,12 @@
 
     @pl.when(jnp.logical_not(w_self))
     def _():
-        copy(w_ref, wbuf.at[w_piece], WGT, {"tm": z}).wait_send()
+        copy(w_ref, wbuf.at[w_piece], WGT + 8, {"tm": z}).wait_send()
+
+    @pl.when(w_home)
+    def _():
+        for r in range(1, NDP):
+            copy(wbuf, wbuf, WGT + 9 + r, {"dp": ahead(d, r, NDP)}, WGT + 9).wait_send()
 
 
 def shards(latents, owner, gamma, beta, weight, upstream):
@@ -525,10 +527,10 @@
         ((NTM, 8, GS, CELLS), BF16),
         ((2, TILES, CELLS, 128), BF16),
         ((2, NSP, CAP, CELLS, 128), BF16),
-        ((8, 128), F32),
-        ((NDP, 8, 128), F32),
-        ((8, 128), F32),
-        ((NTM, NSP, 8, 128), F32),
+        ((2, 128), F32),
+        ((NDP, 2, 128), F32),
+        ((2, 128), F32),
+        ((NTM, NSP, 2, 128), F32),
     ]
     dlat, dw, dgam, dbet = pl.pallas_call(
         body,

time: 89.5 us -> 77.6 us (0.87); the launches traced: 88.3 us -> 77.4 us
  Pallas kernels: 83.9 us -> 73 us
    pallas_call x1, Pallas kernels: 83.9 us -> 73 us  [shards(): pl.pallas_call(body, out_shape=(jax.ShapeDtypeStruct((2, CAP, CELLS, C),...]
where the time goes in v3:
time: 77.6 us; the launch traced here: 77.4 us
  Pallas kernels  73 us (94%)
  local copies, waits for them, and re-layouts  3.77 us (5%)
    pallas_call x1, Pallas kernels, shards(): pl.pallas_call(body, out_shape=(jax.ShapeDtypeStruct((2, CAP, CELLS, C),...  73 us
    unnamed x10, local copies, waits for them, and re-layouts  3.77 us

profile of v3, /device:TPU:1, one launch (start us, length us, event | category | flops | bytes accessed | tf_op | source)
XLA Modules:
  0.0 77.4 jit_solution(2742101583591229418)
XLA Ops:
  0.6 73.0 %shard_map.93 = (bf16[2,2,128,512]{3,2,1,0:T(8,128)(2,1)}, f32[27,2,256]{2,1,0:T(2,128)}, f32[4,128]{1,0:T(4,128)}, f32[4,128]{1,0:T(4,128)}) custom-call(s32[4]{0:T(128)} %bitcast.19, f32[4,128]{1,0:T(4,128)} %bitcast.15, f32[4,128]{1,0:T(4,128)} %bitcast.16, bf16[2,2,128,512]{3,2,1,0:T(8,128)(2,1)} %bitcast.10, bf16[2,512,256]{2,1,0:T(8,128)(2,1)} %bitcast.11, ...), custom_call_target="tpu_custom_call" | custom-call | tf_op jit(solution)/shard_map/pallas_call | solution.py:535
  73.6 0.0 copy-start
  73.6 1.9 %copy.14 = bf16[1,2,2,128,512]{4,3,2,1,0:T(8,128)(2,1)} copy(bf16[1,2,2,128,512]{4,3,2,1,0:T(8,128)(2,1)} %bitcast.12) | data formatting | bytes 1048576
  75.5 0.0 copy-done
  75.5 0.0 copy-start.2
  75.5 0.6 copy.15
  76.2 0.0 copy-done.2
  76.2 0.0 copy-start.1
  76.2 0.6 copy.16
  76.7 0.1 copy-done.1
  76.8 0.6 copy.17
Async XLA Ops:
  73.6 1.9 %copy-start = (f32[27,2,256]{2,1,0:T(2,128)S(1)}, f32[27,2,256]{2,1,0:T(2,128)}, u32[]{:S(2)}) copy-start(f32[27,2,256]{2,1,0:T(2,128)} %get-tuple-element.9) | copy-start | bytes 165892
  75.5 0.6 copy-start.2
  76.2 0.7 copy-start.1

commit v4 on v3

--- a/solution.py
+++ b/solution.py
@@ -41,9 +41,11 @@
     ahead = lambda v, r, n: lax.rem(v + r, n)
     behind = lambda v, r, n: lax.rem(v - r + n, n)
     line = (d * NTM + z) * NSP + y
-    mine = y * NTM + z
+    place = lambda v: 4 * lax.rem(v, 2) + v // 2
+    tz = place(z)
+    mine = y * NTM + tz
     w_group = line // 8
-    w_tm, w_sp = lax.rem(w_group, NTM), w_group // NTM
+    w_tm, w_sp = 2 * lax.rem(w_group, 4) + lax.rem(w_group, NTM) // 4, w_group // NTM
     w_piece = lax.rem(line, 8)
     src = lambda i: {
         "dp": mine // 4,
@@ -52,7 +54,6 @@
     }
     w_self = (w_tm == z) & (w_sp == y)
     w_home = d == mine // 4
-    own_piece_here = line // 8 == mine
 
     started = []
 
@@ -76,15 +77,14 @@
     def greet(to):
         pl.semaphore_signal(barrier, inc=1, device_id=to, device_id_type=MESH)
 
-    for r in range(NTM):
-        for q in range(NSP):
-            if r or q:
-                greet({"tm": ahead(z, r, NTM), "space": ahead(y, q, NSP)})
+    pair = z + 1 - 2 * lax.rem(z, 2)
+    for r in range(1, NSP):
+        greet({"space": ahead(y, r, NSP)})
+        greet({"tm": pair, "space": ahead(y, r, NSP)})
+    greet({"tm": ahead(z, 1, NTM)})
+    greet({"tm": behind(z, 1, NTM)})
     for r in range(1, NDP):
         greet({"dp": ahead(d, r, NDP)})
-    @pl.when(jnp.logical_not(own_piece_here & (w_piece == d)))
-    def _():
-        greet({"dp": w_piece, "tm": w_tm, "space": w_sp})
 
     p = lax.broadcasted_iota(jnp.int32, (CELLS, 4 * CELLS), 0)
     q = lax.broadcasted_iota(jnp.int32, (CELLS, 4 * CELLS), 1)
@@ -98,7 +98,7 @@
 
     own_to = 8 * mine + d
     self_t = jnp.where(own_to == line, 1, 0)
-    pl.semaphore_wait(barrier, NTM * NSP - 1 + NDP - 1 + 1 - self_t)
+    pl.semaphore_wait(barrier, 2 * (NSP - 1) + 2 + NDP - 1)
 
     def part_b(zo, yo, f=0, n=2):
         return gz.at[pl.ds(2 * zo + f, n), yo, pl.ds(LEFT, CELLS - LEFT)]
@@ -280,8 +280,8 @@
             zsend[:, f * TILES + t] = v.T.reshape(NTM, GS, CELLS).astype(BF16)
     for r in range(1, NTM):
         zo = ahead(z, r, NTM)
-        go(zsend.at[zo], xbuf.at[z], L_TM + r, {"tm": zo})
-    xbuf[z] = zsend[z]
+        go(zsend.at[place(zo)], xbuf.at[z], L_TM + r, {"tm": zo})
+    xbuf[z] = zsend[tz]
 
     @pl.when(jnp.logical_not(w_home))
     def _():
@@ -323,7 +323,7 @@
 
     row16 = lax.broadcasted_iota(jnp.int32, (GS, CELLS), 0)
     lane16 = lax.broadcasted_iota(jnp.int32, (GS, CELLS), 1)
-    diag = lane16 == z * GS + row16
+    diag = lane16 == tz * GS + row16
 
     def column(ref):
         return jnp.sum(jnp.where(diag, ref[pl.ds(y, 1), :], 0.0), axis=1, keepdims=True)
@@ -403,8 +403,8 @@
     for f in range(2):
         for r in range(1, NTM):
             zo = ahead(z, r, NTM)
-            go(of_frame(dxs, zo, f), of_frame(zback, z, f), D_TM + 8 * f + r, {"tm": zo})
-    zback[z] = dxs[z]
+            go(of_frame(dxs, zo, f), of_frame(zback, tz, f), D_TM + 8 * f + r, {"tm": zo})
+    zback[tz] = dxs[z]
 
     gown[0:1, :] = jnp.sum(jnp.where(diag, dgam * rscale, 0.0), axis=0, keepdims=True)
     gown[1:2, :] = jnp.sum(jnp.where(diag, dbet * rscale, 0.0), axis=0, keepdims=True)
@@ -417,7 +417,7 @@
 
     def to_slots(f):
         for r in range(1, NTM):
-            got(of_frame(zback, behind(z, r, NTM), f), D_TM + 8 * f + r)
+            got(of_frame(zback, place(behind(z, r, NTM)), f), D_TM + 8 * f + r)
         for t in range(TILES):
             v = zback[:, f * TILES + t].astype(F32).reshape(NTM * GS, CELLS)
             tback[f, t] = v.T.astype(BF16)
@@ -501,6 +501,11 @@
     def _():
         for r in range(1, NDP):
             copy(wbuf, wbuf, WGT + 9 + r, {"dp": ahead(d, r, NDP)}, WGT + 9).wait_send()
+
+
+def written(*refs):
+    for a, b in zip(refs[:4], refs[4:]):
+        b[...] = a[...]
 
 
 def shards(latents, owner, gamma, beta, weight, upstream):
@@ -559,6 +564,12 @@
         upstream.reshape(2, 4 * CELLS, COUT),
         weight.transpose(1, 0, 2),
     )
+    dlat, dw, dgam, dbet = pl.pallas_call(
+        written,
+        out_shape=[jax.ShapeDtypeStruct(v.shape, v.dtype) for v in (dlat, dw, dgam, dbet)],
+        in_specs=[vmem] * 4,
+        out_specs=[vmem] * 4,
+    )(dlat, dw, dgam, dbet)
     return dlat[None], dw.transpose(1, 0, 2), dgam.reshape(C), dbet.reshape(C)
 
 

time: 77.6 us -> 72.9 us (0.939); the launches traced: 77.4 us -> 71.8 us
  local copies, waits for them, and re-layouts: 3.77 us -> 0 us
  Pallas kernels: 73 us -> 71.2 us
    unnamed x10 -> x0, local copies, waits for them, and re-layouts: 3.77 us -> none
    pallas_call x1, Pallas kernels: 73 us -> 69.3 us  [shards(): pl.pallas_call(body, out_shape=(jax.ShapeDtypeStruct((2, CAP, CELLS, C),...]
    pallas_call x0 -> x1, Pallas kernels: none -> 1.92 us  [shards(): pl.pallas_call(written, out_shape=[jax.ShapeDtypeStruct(v.shape, v.dtype)...]
where the time goes in v4:
time: 72.9 us; the launch traced here: 71.8 us
  Pallas kernels  71.2 us (98%)
    pallas_call x1, Pallas kernels, shards(): pl.pallas_call(body, out_shape=(jax.ShapeDtypeStruct((2, CAP, CELLS, C),...  69.3 us
    pallas_call x1, Pallas kernels, shards(): pl.pallas_call(written, out_shape=[jax.ShapeDtypeStruct(v.shape, v.dtype)...  1.92 us

profile of v4, /device:TPU:1, one launch (start us, length us, event | category | flops | bytes accessed | tf_op | source)
XLA Modules:
  0.0 71.8 jit_solution(16113101883730661260)
XLA Ops:
  0.6 69.3 %shard_map.93 = (bf16[2,2,128,512]{3,2,1,0:T(8,128)(2,1)}, f32[27,2,256]{2,1,0:T(2,128)}, f32[4,128]{1,0:T(4,128)}, f32[4,128]{1,0:T(4,128)}) custom-call(s32[4]{0:T(128)} %bitcast.15, f32[4,128]{1,0:T(4,128)} %bitcast.13, f32[4,128]{1,0:T(4,128)} %bitcast.14, bf16[2,2,128,512]{3,2,1,0:T(8,128)(2,1)} %bitcast.10, bf16[2,512,256]{2,1,0:T(8,128)(2,1)} %bitcast.11, ...), custom_call_target="tpu_custom_call" | custom-call | tf_op jit(solution)/shard_map/pallas_call | solution.py:540
  69.9 1.9 %shard_map.94 = (bf16[2,2,128,512]{3,2,1,0:T(8,128)(2,1)}, f32[27,2,256]{2,1,0:T(2,128)}, f32[4,128]{1,0:T(4,128)}, f32[4,128]{1,0:T(4,128)}) custom-call(bf16[2,2,128,512]{3,2,1,0:T(8,128)(2,1)} %get-tuple-element.12.refs_0_, f32[27,2,256]{2,1,0:T(2,128)} %get-tuple-element.13.refs_1_, f32[4,128]{1,0:T(4,128)} %get-tuple-element.14.refs_2_, ...), custom_call_target="tpu_custom_call" | custom-call | tf_op jit(solution)/shard_map/pallas_call | solution.py:567

commit v5 on v4

--- a/solution.py
+++ b/solution.py
@@ -27,15 +27,16 @@
 
 B_TM, B_SP, A_SP, A_TM = 0, 8, 40, 44
 L_SP, L_TM, WGT = 76, 80, 88
-D_TM, D_DP, G_DP, D_SP, D_OWN, G_ALL = 112, 128, 136, 144, 152, 153
-N_SEM = 185
+D_TM, D_DP, G_DP, D_SP, D_OWN, G_ALL = 112, 120, 136, 144, 176, 178
+N_SEM = 210
+HALVES = ((0, 14), (14, TAPS - 14))
 
 
 def body(
     owner_ref, gamma_ref, beta_ref, lat_ref, ups_ref, w_ref,
-    dlat_ref, dw_ref, dgam_ref, dbet_ref,
+    slab_ref, dw_ref, dgam_ref, dbet_ref,
     gz, ybuf, zsend, xbuf, wbuf, wf, wall, a9, xh, ds, dhb, rsd, dk, dsend, drecv, dsum,
-    dxs, zback, tback, ysend, gown, gdp, gsum, gall, send_sem, recv_sem, own_sem,
+    dxs, zback, ysend, gown, gdp, gsum, gall, send_sem, recv_sem, own_sem,
 ):
     d, z, y = lax.axis_index("dp"), lax.axis_index("tm"), lax.axis_index("space")
     ahead = lambda v, r, n: lax.rem(v + r, n)
@@ -371,9 +372,12 @@
     rscale = 1.0 / math.sqrt(NDP * FR * TILES * CELLS)
     for i in range(8):
         dsend[i] = dk[:, 2 * i : 2 * i + 2, :] * rscale
-    for r in range(1, NDP):
-        to = ahead(d, r, NDP)
-        go(dsend.at[to], drecv.at[d], D_DP + r, {"dp": to})
+    for h, (k0, kn) in enumerate(HALVES):
+        for r in range(1, NDP):
+            to = ahead(d, r, NDP)
+            go(
+                dsend.at[to, pl.ds(k0, kn)], drecv.at[d, pl.ds(k0, kn)], D_DP + 8 * h + r, {"dp": to}
+            )
     drecv[d] = dsend[d]
 
     dhidden(4)
@@ -397,13 +401,9 @@
 
     lax.fori_loop(0, NTM, dinput, 0)
 
-    def of_frame(ref, i, f):
-        return ref.at[i, pl.ds(f * TILES, TILES)]
-
-    for f in range(2):
-        for r in range(1, NTM):
-            zo = ahead(z, r, NTM)
-            go(of_frame(dxs, zo, f), of_frame(zback, tz, f), D_TM + 8 * f + r, {"tm": zo})
+    for r in range(1, NTM):
+        zo = ahead(z, r, NTM)
+        go(dxs.at[zo], zback.at[tz], D_TM + r, {"tm": zo})
     zback[tz] = dxs[z]
 
     gown[0:1, :] = jnp.sum(jnp.where(diag, dgam * rscale, 0.0), axis=0, keepdims=True)
@@ -413,30 +413,31 @@
         go(gown, gdp.at[d], G_DP + r, {"dp": to})
     gdp[d] = gown[...]
 
-    lanes = pl.ds(pl.multiple_of(y * 128, 128), 128)
-
-    def to_slots(f):
-        for r in range(1, NTM):
-            got(of_frame(zback, place(behind(z, r, NTM)), f), D_TM + 8 * f + r)
-        for t in range(TILES):
-            v = zback[:, f * TILES + t].astype(F32).reshape(NTM * GS, CELLS)
-            tback[f, t] = v.T.astype(BF16)
+    held = []
+    for yo in range(NSP):
+        for j in range(CAP):
+            held.append([(owners[t] == yo) & (ranks[t] == j) for t in range(TILES)])
+    nearest = (0, 1, 7, 2, 6, 3, 5, 4)
+
+    def to_slots(k):
+        r = nearest[k]
+        p = place(behind(z, r, NTM))
+        if r:
+            got(zback.at[p], D_TM + r)
+        tiles = [zback[p, i] for i in range(2 * TILES)]
         for yo in range(NSP):
             for j in range(CAP):
-                tile, live = jnp.int32(0), jnp.int32(0)
-                for t in range(TILES):
-                    here = (owners[t] == yo) & (ranks[t] == j)
-                    tile, live = jnp.where(here, t, tile), jnp.where(here, 1, live)
-                v = tback[f, tile]
-                ysend[f, yo, j] = jnp.where(live > 0, v, jnp.zeros_like(v))
+                for f in range(2):
+                    v = jnp.zeros((GS, CELLS), BF16)
+                    for t in range(TILES):
+                        v = jnp.where(held[CAP * yo + j][t], tiles[f * TILES + t], v)
+                    ysend[p, yo, f, j] = v
         for r in range(1, NSP):
             yo = ahead(y, r, NSP)
-            go(ysend.at[f, yo], dlat_ref.at[f, :, :, lanes], D_SP + 4 * f + r, {"space": yo})
-        own = pltpu.make_async_copy(ysend.at[f, y], dlat_ref.at[f, :, :, lanes], own_sem.at[1 + f])
-        own.start()
-        return own
-
-    owns = [to_slots(0)]
+            go(ysend.at[p, yo], slab_ref.at[y, p], D_SP + 4 * k + r, {"space": yo})
+
+    for k in range(3):
+        to_slots(k)
 
     for r in range(1, NDP):
         got(gdp.at[behind(d, r, NDP)], G_DP + r)
@@ -451,23 +452,28 @@
                 go(gsum, gall.at[z, y], G_ALL + r * NSP + q, to)
     gall[z, y] = gsum[...]
 
-    owns.append(to_slots(1))
-
-    for r in range(1, NDP):
-        got(drecv.at[behind(d, r, NDP)], D_DP + r)
-    acc = drecv[0]
-    for i in range(1, NDP):
-        acc = acc + drecv[i]
-    dsum[...] = acc
-    to_owner = copy(dsum, dw_ref, D_OWN, src(d))
-
-    @pl.when(self_t == 0)
-    def _():
-        to_owner.start()
-
-    @pl.when(self_t == 1)
-    def _():
-        pltpu.make_async_copy(dsum, dw_ref, recv_sem.at[D_OWN]).start()
+    for k in range(3, NTM):
+        to_slots(k)
+    own = pltpu.make_async_copy(ysend.at[:, y], slab_ref.at[y], own_sem.at[1])
+    own.start()
+
+    for h, (k0, kn) in enumerate(HALVES):
+        half = pl.ds(k0, kn)
+        for r in range(1, NDP):
+            got(drecv.at[behind(d, r, NDP), half], D_DP + 8 * h + r)
+        acc = drecv[0, k0 : k0 + kn]
+        for i in range(1, NDP):
+            acc = acc + drecv[i, k0 : k0 + kn]
+        dsum[k0 : k0 + kn] = acc
+        to_owner = copy(dsum.at[half], dw_ref.at[half], D_OWN + h, src(d))
+
+        @pl.when(self_t == 0)
+        def _():
+            to_owner.start()
+
+        @pl.when(self_t == 1)
+        def _():
+            pltpu.make_async_copy(dsum.at[half], dw_ref.at[half], recv_sem.at[D_OWN + h]).start()
 
     for r in range(NTM):
         for q in range(NSP):
@@ -480,18 +486,21 @@
         dgam_ref[s : s + 1, :] = acc[0:1]
         dbet_ref[s : s + 1, :] = acc[1:2]
 
-    for f in range(2):
-        owns[f].wait()
+    own.wait()
+    for k in range(NTM):
+        p = place(behind(z, nearest[k], NTM))
         for r in range(1, NSP):
-            yo = behind(y, r, NSP)
-            got(dlat_ref.at[f, :, :, pl.ds(pl.multiple_of(yo * 128, 128), 128)], D_SP + 4 * f + r)
-    got(dw_ref, D_OWN)
+            got(slab_ref.at[behind(y, r, NSP), p], D_SP + 4 * k + r)
+    for h, (k0, kn) in enumerate(HALVES):
+        got(dw_ref.at[pl.ds(k0, kn)], D_OWN + h)
     for c in started:
         c.wait_send()
 
     @pl.when(self_t == 0)
     def _():
-        copy(dsum, dw_ref, D_OWN, src(d)).wait_send()
+        for h, (k0, kn) in enumerate(HALVES):
+            half = pl.ds(k0, kn)
+            copy(dsum.at[half], dw_ref.at[half], D_OWN + h, src(d)).wait_send()
 
     @pl.when(jnp.logical_not(w_self))
     def _():
@@ -503,8 +512,13 @@
             copy(wbuf, wbuf, WGT + 9 + r, {"dp": ahead(d, r, NDP)}, WGT + 9).wait_send()
 
 
-def written(*refs):
-    for a, b in zip(refs[:4], refs[4:]):
+def written(slab_ref, *refs):
+    for f in range(2):
+        for j in range(CAP):
+            for q in range(NSP):
+                v = slab_ref[q, :, f, j].astype(F32).reshape(128, CELLS)
+                refs[3][f, j, :, 128 * q : 128 * (q + 1)] = v.T.astype(BF16)
+    for a, b in zip(refs[:3], refs[4:]):
         b[...] = a[...]
 
 
@@ -530,17 +544,16 @@
         ((TAPS, 2, COUT), F32),
         ((NTM, 8, GS, CELLS), BF16),
         ((NTM, 8, GS, CELLS), BF16),
-        ((2, TILES, CELLS, 128), BF16),
-        ((2, NSP, CAP, CELLS, 128), BF16),
+        ((NTM, NSP, 2, CAP, GS, CELLS), BF16),
         ((2, 128), F32),
         ((NDP, 2, 128), F32),
         ((2, 128), F32),
         ((NTM, NSP, 2, 128), F32),
     ]
-    dlat, dw, dgam, dbet = pl.pallas_call(
+    slab, dw, dgam, dbet = pl.pallas_call(
         body,
         out_shape=(
-            jax.ShapeDtypeStruct((2, CAP, CELLS, C), BF16),
+            jax.ShapeDtypeStruct((NSP, NTM, 2, CAP, GS, CELLS), BF16),
             jax.ShapeDtypeStruct((TAPS, 2, COUT), F32),
             jax.ShapeDtypeStruct((4, 128), F32),
             jax.ShapeDtypeStruct((4, 128), F32),
@@ -566,10 +579,11 @@
     )
     dlat, dw, dgam, dbet = pl.pallas_call(
         written,
-        out_shape=[jax.ShapeDtypeStruct(v.shape, v.dtype) for v in (dlat, dw, dgam, dbet)],
+        out_shape=[jax.ShapeDtypeStruct((2, CAP, CELLS, C), BF16)]
+        + [jax.ShapeDtypeStruct(v.shape, v.dtype) for v in (dw, dgam, dbet)],
         in_specs=[vmem] * 4,
         out_specs=[vmem] * 4,
-    )(dlat, dw, dgam, dbet)
+    )(slab, dw, dgam, dbet)
     return dlat[None], dw.transpose(1, 0, 2), dgam.reshape(C), dbet.reshape(C)
 
 

time: 72.9 us -> 72.1 us (0.989); the launches traced: 71.8 us -> 71.9 us
  no operation moved by 1% of the time
where the time goes in v5:
time: 72.1 us; the launch traced here: 71.9 us
  Pallas kernels  71.2 us (99%)
    pallas_call x1, Pallas kernels, shards(): pl.pallas_call(body, out_shape=(jax.ShapeDtypeStruct((NSP, NTM, 2, CAP, G...  69.2 us
    pallas_call x1, Pallas kernels, shards(): pl.pallas_call(written, out_shape=[jax.ShapeDtypeStruct((2, CAP, CELLS, C...  2.09 us

profile of v5, /device:TPU:1, one launch (start us, length us, event | category | flops | bytes accessed | tf_op | source)
XLA Modules:
  0.0 71.9 jit_solution(9712048775880740703)
XLA Ops:
  0.6 69.2 %shard_map.93 = (bf16[4,8,2,2,16,128]{5,4,3,2,1,0:T(8,128)(2,1)}, f32[27,2,256]{2,1,0:T(2,128)}, f32[4,128]{1,0:T(4,128)}, f32[4,128]{1,0:T(4,128)}) custom-call(s32[4]{0:T(128)} %bitcast.15, f32[4,128]{1,0:T(4,128)} %bitcast.13, f32[4,128]{1,0:T(4,128)} %bitcast.14, bf16[2,2,128,512]{3,2,1,0:T(8,128)(2,1)} %bitcast.10, bf16[2,512,256]{2,1,0:T(8,128)(2,1)} %bitcast.11, ...), custom_call_target="tpu_custom_call" | custom-call | tf_op jit(solution)/shard_map/pallas_call | solution.py:553
  69.8 2.1 %shard_map.94 = (bf16[2,2,128,512]{3,2,1,0:T(8,128)(2,1)}, f32[27,2,256]{2,1,0:T(2,128)}, f32[4,128]{1,0:T(4,128)}, f32[4,128]{1,0:T(4,128)}) custom-call(bf16[4,8,2,2,16,128]{5,4,3,2,1,0:T(8,128)(2,1)} %get-tuple-element.12.slab_ref, f32[27,2,256]{2,1,0:T(2,128)} %get-tuple-element.13.refs_0_, f32[4,128]{1,0:T(4,128)} %get-tuple-element.14.refs_1_, ...), custom_call_target="tpu_custom_call" | custom-call | tf_op jit(solution)/shard_map/pallas_call | solution.py:580

commit v6 on v5

--- a/solution.py
+++ b/solution.py
@@ -369,6 +369,32 @@
     complete(4)
     dweight(4)
 
+    dhidden(4)
+    dhb[8:12] = dhb[8:12] + (dhb[0:4] + dhb[4:8])
+
+    def gains(i, acc):
+        dact = dhb[pl.ds(8 + 8 * i, 8)] * ds[i]
+        dhb[pl.ds(8 + 8 * i, 8)] = dact
+        return acc[0] + jnp.sum(dact * xh[i], axis=0), acc[1] + jnp.sum(dact, axis=0)
+
+    dgam, dbet = lax.fori_loop(0, NTM, gains, (zero, zero))
+    dgam = jnp.sum(dgam, axis=1, keepdims=True)
+    dbet = jnp.sum(dbet, axis=1, keepdims=True)
+    m1 = jnp.sum(dbet * gamma, axis=0, keepdims=True) / count
+    m2 = jnp.sum(dgam * gamma, axis=0, keepdims=True) / count
+
+    def dinput(i, _):
+        v = inverse * (dhb[pl.ds(8 + 8 * i, 8)] * gamma - m1 - xh[i] * m2)
+        dxs[i] = (v + rsd[pl.ds(8 * i, 8)]).astype(BF16)
+        return 0
+
+    lax.fori_loop(0, NTM, dinput, 0)
+
+    for r in range(1, NTM):
+        zo = ahead(z, r, NTM)
+        go(dxs.at[zo], zback.at[tz], D_TM + r, {"tm": zo})
+    zback[tz] = dxs[z]
+
     rscale = 1.0 / math.sqrt(NDP * FR * TILES * CELLS)
     for i in range(8):
         dsend[i] = dk[:, 2 * i : 2 * i + 2, :] * rscale
@@ -379,32 +405,6 @@
                 dsend.at[to, pl.ds(k0, kn)], drecv.at[d, pl.ds(k0, kn)], D_DP + 8 * h + r, {"dp": to}
             )
     drecv[d] = dsend[d]
-
-    dhidden(4)
-    dhb[8:12] = dhb[8:12] + (dhb[0:4] + dhb[4:8])
-
-    def gains(i, acc):
-        dact = dhb[pl.ds(8 + 8 * i, 8)] * ds[i]
-        dhb[pl.ds(8 + 8 * i, 8)] = dact
-        return acc[0] + jnp.sum(dact * xh[i], axis=0), acc[1] + jnp.sum(dact, axis=0)
-
-    dgam, dbet = lax.fori_loop(0, NTM, gains, (zero, zero))
-    dgam = jnp.sum(dgam, axis=1, keepdims=True)
-    dbet = jnp.sum(dbet, axis=1, keepdims=True)
-    m1 = jnp.sum(dbet * gamma, axis=0, keepdims=True) / count
-    m2 = jnp.sum(dgam * gamma, axis=0, keepdims=True) / count
-
-    def dinput(i, _):
-        v = inverse * (dhb[pl.ds(8 + 8 * i, 8)] * gamma - m1 - xh[i] * m2)
-        dxs[i] = (v + rsd[pl.ds(8 * i, 8)]).astype(BF16)
-        return 0
-
-    lax.fori_loop(0, NTM, dinput, 0)
-
-    for r in range(1, NTM):
-        zo = ahead(z, r, NTM)
-        go(dxs.at[zo], zback.at[tz], D_TM + r, {"tm": zo})
-    zback[tz] = dxs[z]
 
     gown[0:1, :] = jnp.sum(jnp.where(diag, dgam * rscale, 0.0), axis=0, keepdims=True)
     gown[1:2, :] = jnp.sum(jnp.where(diag, dbet * rscale, 0.0), axis=0, keepdims=True)

time: 72.1 us -> 73.2 us (1.015)
  Pallas kernels: 71.2 us -> 72.5 us
    pallas_call x1, Pallas kernels: 69.2 us -> 70.4 us  [shards(): pl.pallas_call(body, out_shape=(jax.ShapeDtypeStruct((NSP, NTM, 2, CAP, G...]
where the time goes in v6:
time: 73.2 us; the launch traced here: 73.1 us
  Pallas kernels  72.5 us (99%)
    pallas_call x1, Pallas kernels, shards(): pl.pallas_call(body, out_shape=(jax.ShapeDtypeStruct((NSP, NTM, 2, CAP, G...  70.4 us
    pallas_call x1, Pallas kernels, shards(): pl.pallas_call(written, out_shape=[jax.ShapeDtypeStruct((2, CAP, CELLS, C...  2.09 us

profile of v6, /device:TPU:1, one launch (start us, length us, event | category | flops | bytes accessed | tf_op | source)
XLA Modules:
  0.0 73.1 jit_solution(5754132192819721808)
XLA Ops:
  0.6 70.4 %shard_map.93 = (bf16[4,8,2,2,16,128]{5,4,3,2,1,0:T(8,128)(2,1)}, f32[27,2,256]{2,1,0:T(2,128)}, f32[4,128]{1,0:T(4,128)}, f32[4,128]{1,0:T(4,128)}) custom-call(s32[4]{0:T(128)} %bitcast.15, f32[4,128]{1,0:T(4,128)} %bitcast.13, f32[4,128]{1,0:T(4,128)} %bitcast.14, bf16[2,2,128,512]{3,2,1,0:T(8,128)(2,1)} %bitcast.10, bf16[2,512,256]{2,1,0:T(8,128)(2,1)} %bitcast.11, ...), custom_call_target="tpu_custom_call" | custom-call | tf_op jit(solution)/shard_map/pallas_call | solution.py:553
  71.0 2.1 %shard_map.94 = (bf16[2,2,128,512]{3,2,1,0:T(8,128)(2,1)}, f32[27,2,256]{2,1,0:T(2,128)}, f32[4,128]{1,0:T(4,128)}, f32[4,128]{1,0:T(4,128)}) custom-call(bf16[4,8,2,2,16,128]{5,4,3,2,1,0:T(8,128)(2,1)} %get-tuple-element.12.slab_ref, f32[27,2,256]{2,1,0:T(2,128)} %get-tuple-element.13.refs_0_, f32[4,128]{1,0:T(4,128)} %get-tuple-element.14.refs_1_, ...), custom_call_target="tpu_custom_call" | custom-call | tf_op jit(solution)/shard_map/pallas_call | solution.py:580
